TPU v7x, 32 devices: a whole 2x2x4 slice. The times are simulated.
32 devices in a mesh: depth: 2 (over y), lat: 16 (over z, x, core).
Axes of the slice: x: 2, y: 2, z: 4, core: 2. Of those that a mesh axis runs over, the one named last changes fastest.
Arguments:
- source_field: bfloat16 [2, 2, 128, 2048], P(None, None, 'lat'), may hold values from -6 to 6
- receiver_field: bfloat16 [2, 2, 128, 2048], P(None, None, 'lat'), may hold values from -6 to 6
- freq_index: int32 [2], replicated, may hold values from 0 to 63
- slowness: float32 [2, 128, 2048], P('depth', 'lat'), may hold values from 0.5 to 2
- ffd_coef: float32 [2, 128, 2048], P('depth', 'lat'), may hold values from 0.04 to 0.12
- band: bfloat16 [16, 3, 128, 128], P('depth'), may hold values from -0.3125 to 0.3125
- image_mask: int32 [2, 128, 2048], P('depth', 'lat'), may hold values 0 or 1
Outputs:
- image: float32 [2, 128, 2048], P('depth', 'lat')
- gradient: float32 [2, 128, 2048], P('depth', 'lat')
All inputs are finite; a program needn't handle non-finite values. No bound on the sum of `image_mask` on one device may be relied on, other than what follows from the above.
Results may differ from a plain program's by a relative error of at most 0.0035.
The roundings to bfloat16 on the way count: a program that leaves them out, or rounds other values in their place, can miss the bound.
Values may be sent and summed in bfloat16 or wider, within the bound.
A program may use at most 64 MiB of HBM per device.

v0:
```python
import jax
import jax.numpy as jnp
from jax import lax
from jax.sharding import PartitionSpec as P

HALO = 8


def with_halo(value, sides, width):
    for axis, dim in sides:
        size, length = (lax.axis_size(axis), value.shape[dim])
        up = [(i, (i + 1) % size) for i in range(size - 1)]
        down = [(j, i) for i, j in up]
        last = lax.slice_in_dim(value, length - width, length, axis=dim)
        initial = lax.slice_in_dim(value, 0, width, axis=dim)
        before = lax.ppermute(last, axis, up)
        after = lax.ppermute(initial, axis, down)
        value = jnp.concatenate([before, value, after], axis=dim)
    return value


def passed_along(block, axis, distance):
    devices = range(lax.axis_size(axis))
    route = [(i - distance, i) for i in devices if i - distance in devices]
    return lax.ppermute(block, axis, route)


def stencil_rows(rows, padded):
    height = rows.shape[1]
    centre = rows.astype(jnp.float32)
    total = jnp.zeros_like(centre)
    for offset in range(1, HALO + 1):
        upper = lax.slice_in_dim(padded, HALO + offset, HALO + offset + height, axis=1).astype(
            jnp.float32
        )
        lower = lax.slice_in_dim(padded, HALO - offset, HALO - offset + height, axis=1).astype(
            jnp.float32
        )
        total = total + 0.25 / offset * (upper + lower - 2.0 * centre)
    return total


def band_product(rows, band):
    count, height, width = rows.shape
    nblocks = band.shape[0]
    block = band.shape[2]
    tiles = rows.reshape(count, height, nblocks, block)
    padded = jnp.pad(tiles, ((0, 0), (0, 0), (1, 1), (0, 0)))
    total = jnp.zeros(tiles.shape, jnp.float32)
    for offset in range(3):
        window = lax.slice_in_dim(padded, offset, offset + nblocks, axis=2)
        total = total + jnp.einsum(
            "acjb,jbd->acjd", window, band[:, offset], preferred_element_type=jnp.float32
        )
    return total.reshape(count, height, width)


def band_product_t(rows, band):
    count, height, width = rows.shape
    nblocks = band.shape[0]
    block = band.shape[2]
    tiles = rows.reshape(count, height, nblocks, block)
    total = jnp.zeros(tiles.shape, jnp.float32)
    for offset in range(3):
        moved = jnp.einsum(
            "acjd,jbd->acjb", tiles, band[:, offset], preferred_element_type=jnp.float32
        )
        padded = jnp.pad(moved, ((0, 0), (0, 0), (1, 1), (0, 0)))
        total = total + lax.slice_in_dim(padded, 2 - offset, 2 - offset + nblocks, axis=2)
    return total.reshape(count, height, width)


def advance(fields, omegas, slow, coef, band):
    members, comps, height, width = fields.shape
    theta = omegas[:, None, None] * slow[None]
    cosine = jnp.cos(theta)
    sine_part = jnp.sin(theta)
    phase_re = fields[:, 0] * cosine - fields[:, 1] * sine_part
    phase_im = fields[:, 0] * sine_part + fields[:, 1] * cosine
    phased = jnp.stack([phase_re, phase_im], axis=1)
    rows = phased.astype(jnp.bfloat16).reshape(members * comps, height, width)
    padded = with_halo(rows, (("lat", 1),), HALO)
    lateral = (band_product(rows, band) + stencil_rows(rows, padded)).reshape(
        members, comps, height, width
    )
    stepped = jnp.stack([phase_re - coef * lateral[:, 1], phase_im + coef * lateral[:, 0]], axis=1)
    return (phased, stepped)


def retreat(adjoint, phased, omegas, slow, coef, band):
    members, comps, height, width = adjoint.shape
    scaled = (coef * adjoint).astype(jnp.bfloat16).reshape(members * comps, height, width)
    padded = with_halo(scaled, (("lat", 1),), HALO)
    lateral = (band_product_t(scaled, band) + stencil_rows(scaled, padded)).reshape(
        members, comps, height, width
    )
    back_re = adjoint[:, 0] + lateral[:, 1]
    back_im = adjoint[:, 1] - lateral[:, 0]
    weights = omegas[:, None, None]
    term = jnp.sum(weights * (back_im * phased[:, 0] - back_re * phased[:, 1]), axis=0)
    theta = weights * slow[None]
    cosine = jnp.cos(theta)
    sine_part = jnp.sin(theta)
    upward = jnp.stack(
        [back_re * cosine + back_im * sine_part, back_im * cosine - back_re * sine_part], axis=1
    )
    return (term, upward)


def per_device(source_field, receiver_field, freq_index, slowness, ffd_coef, band, image_mask):
    position = lax.axis_index("depth")
    sections = lax.axis_size("depth")
    count = source_field.shape[0]
    layers = slowness.shape[0]
    height = slowness.shape[1]
    width = slowness.shape[2]
    omega_all = 0.1 * (freq_index.astype(jnp.float32) + 1.0)
    band = lax.all_gather(band, "depth", axis=0, tiled=True)
    ticks = count + sections - 1
    store_shape = (layers, count, 2, height, width)

    def fore_tick(tick, carry):
        inflow, image_acc, keep_s, keep_p = carry
        micro = tick - position
        active_tick = (micro >= 0) & (micro < count)
        micro_slot = jnp.clip(micro, 0, count - 1)
        first_src = lax.dynamic_index_in_dim(source_field, micro_slot, 0, keepdims=False)
        first_rcv = lax.dynamic_index_in_dim(receiver_field, micro_slot, 0, keepdims=False)
        entering = jnp.where(position == 0, jnp.stack([first_src, first_rcv]), inflow)
        fields = entering.astype(jnp.float32)
        omega_one = lax.dynamic_slice_in_dim(omega_all, micro_slot, 1)
        omega_pair = jnp.concatenate([omega_one, omega_one])
        phased, fields = advance(fields, omega_pair, slowness[0], ffd_coef[0], band)
        product = jnp.sum(fields[0] * fields[1], axis=0)
        image_acc = image_acc.at[0].add(jnp.where(active_tick, product, 0.0))
        keep_s = keep_s.at[0, micro_slot].set(
            jnp.where(active_tick, fields[0], keep_s[0, micro_slot])
        )
        keep_p = keep_p.at[0, micro_slot].set(
            jnp.where(active_tick, phased[1], keep_p[0, micro_slot])
        )
        outflow = fields.astype(jnp.bfloat16)
        inflow = passed_along(outflow, "depth", 1)
        return (inflow, image_acc, keep_s, keep_p)

    start = (
        jnp.zeros((2, 2, height, width), jnp.bfloat16),
        jnp.zeros((layers, height, width), jnp.float32),
        jnp.zeros(store_shape, jnp.float32),
        jnp.zeros(store_shape, jnp.float32),
    )
    unused, image_acc, keep_s, keep_p = lax.fori_loop(0, ticks, fore_tick, start)
    image = image_acc / count
    masked = image_mask.astype(jnp.float32) * image

    def back_tick(tick, carry):
        inflow, grad_acc = carry
        micro = tick - (sections - 1 - position)
        active_tick = (micro >= 0) & (micro < count)
        micro_slot = jnp.clip(micro, 0, count - 1)
        adjoint = jnp.where(position == sections - 1, 0.0, inflow.astype(jnp.float32))
        omega_one = lax.dynamic_slice_in_dim(omega_all, micro_slot, 1)
        for level in reversed(range(layers)):
            adjoint = adjoint + (masked[level] * keep_s[level, micro_slot])[None]
            term, adjoint = retreat(
                adjoint,
                keep_p[level, micro_slot][None],
                omega_one,
                slowness[level],
                ffd_coef[level],
                band,
            )
            grad_acc = grad_acc.at[level].add(jnp.where(active_tick, term, 0.0))
        inflow = passed_along(adjoint.astype(jnp.bfloat16), "depth", -1)
        return (inflow, grad_acc)

    start_back = (
        jnp.zeros((1, 2, height, width), jnp.bfloat16),
        jnp.zeros((layers, height, width), jnp.float32),
    )
    unused_flow, grad_acc = lax.fori_loop(0, ticks, back_tick, start_back)
    gradient = grad_acc / count
    return (image, gradient)


def solution(mesh):
    return jax.shard_map(
        per_device,
        mesh=mesh,
        in_specs=(
            P(None, None, "lat", None),
            P(None, None, "lat", None),
            P(),
            P("depth", "lat", None),
            P("depth", "lat", None),
            P("depth", None, None, None),
            P("depth", "lat", None),
        ),
        out_specs=(P("depth", "lat", None), P("depth", "lat", None)),
        check_vma=False,
    )
```

profile of v0, /device:TPU:8, one launch (start us, length us, event | category | flops | bytes accessed | tf_op | source)
XLA Modules:
  0.0 160.2 jit_solution(17111445324272083314)
XLA Ops:
  7.3 2.2 %copy.20 = bf16[8,3,128,128]{3,2,0,1:T(8,128)(2,1)} copy(bf16[8,3,128,128]{3,2,1,0:T(8,128)(2,1)} %param.24) | data formatting | bytes 1572864 | tf_op args[5]
  9.6 28.5 %all-gather.2.cloned.1.call-done = bf16[16,3,128,128]{3,2,0,1:T(8,128)(2,1)} async-done(((bf16[8,3,128,128]{3,2,0,1:T(8,128)(2,1)}), bf16[16,3,128,128]{3,2,0,1:T(8,128)(2,1)}) %all-gather.2.cloned.1.call-update) | async-done | bytes 1572880 | tf_op jit(solution)/shard_map/all_gather | solution.py:118
  38.2 56.1 %while.46 = (s32[]{:T(128)}, bf16[2,2,8,2048]{3,2,1,0:T(8,128)(2,1)S(1)}, f32[1,8,2048]{2,1,0:T(8,128)S(1)}, f32[1,2,2,8,2048]{4,3,2,1,0:T(8,128)S(1)}, f32[1,2,...) while((s32[]{:T(128)}, ...), condition=%wide.region_3.4_spmd.clone, body=%wide.region_0.3_spmd.clone.sunk | while | flops 55443484 | bytes 16908796 | solution.py:152
  40.3 1.9 %collective-permute-start = (bf16[4,8,2048]{2,1,0:T(8,128)(2,1)S(1)}, bf16[4,8,2048]{2,1,0:T(8,128)(2,1)S(1)}, u32[]{:S(2)}, u32[]{:S(2)}) collective-permute-start(bf16[4,8,2048]{2,1,0:T(8,128)(2,1)S(1)} %bitcast.181), channel_id=1, source_target_pairs={{0,1},{1,2},{2,3},{3,4},{4,5},{5,6},{6,7},{7,8},{8,9},{9,10},{10,1... | collective-permute-start | bytes 393224 | tf_op jit(solution)/shard_map/while/body/eval_jaxpr/ppermute | solution.py:16
  42.2 4.5 %collective-permute-start.1 = (bf16[4,8,2048]{2,1,0:T(8,128)(2,1)S(1)}, bf16[4,8,2048]{2,1,0:T(8,128)(2,1)S(1)}, u32[]{:S(2)}, u32[]{:S(2)}) collective-permute-start(bf16[4,8,2048]{2,1,0:T(8,128)(2,1)S(1)} %bitcast.182), channel_id=1, source_target_pairs={{1,0},{2,1},{3,2},{4,3},{5,4},{6,5},{7,6},{8,7},{9,8},{10,9},{11,1... | collective-permute-start | bytes 393224 | tf_op jit(solution)/shard_map/while/body/eval_jaxpr/ppermute | solution.py:17
  50.2 2.5 %collective-permute-start.2 = (bf16[2,2,8,2048]{3,2,1,0:T(8,128)(2,1)S(1)}, bf16[2,2,8,2048]{3,2,1,0:T(8,128)(2,1)S(1)}, u32[]{:S(2)}, u32[]{:S(2)}) collective-permute-start(bf16[2,2,8,2048]{3,2,1,0:T(8,128)(2,1)S(1)} %fusion.119), channel_id=1, source_target_pairs={{0,16},{1,17},{2,18},{3,19},{4,20},{5,21},{6,22},{7,23},{8,24},{9,... | collective-permute-start | bytes 393224 | tf_op jit(solution)/shard_map/while/body/eval_jaxpr/ppermute | solution.py:25
  53.5 2.9 %collective-permute-done.2 = bf16[2,2,8,2048]{3,2,1,0:T(8,128)(2,1)S(1)} collective-permute-done((bf16[2,2,8,2048]{3,2,1,0:T(8,128)(2,1)S(1)}, bf16[2,2,8,2048]{3,2,1,0:T(8,128)(2,1)S(1)}, u32[]{:S(2)}, u32[]{:S(2)}) %collective-permute-start.2) | collective-permute-done | bytes 131104 | tf_op jit(solution)/shard_map/while/body/eval_jaxpr/ppermute | solution.py:25
  58.4 1.9 %collective-permute-start = (bf16[4,8,2048]{2,1,0:T(8,128)(2,1)S(1)}, bf16[4,8,2048]{2,1,0:T(8,128)(2,1)S(1)}, u32[]{:S(2)}, u32[]{:S(2)}) collective-permute-start(bf16[4,8,2048]{2,1,0:T(8,128)(2,1)S(1)} %bitcast.181), channel_id=1, source_target_pairs={{0,1},{1,2},{2,3},{3,4},{4,5},{5,6},{6,7},{7,8},{8,9},{9,10},{10,1... | collective-permute-start | bytes 393224 | tf_op jit(solution)/shard_map/while/body/eval_jaxpr/ppermute | solution.py:16
  60.4 4.5 %collective-permute-start.1 = (bf16[4,8,2048]{2,1,0:T(8,128)(2,1)S(1)}, bf16[4,8,2048]{2,1,0:T(8,128)(2,1)S(1)}, u32[]{:S(2)}, u32[]{:S(2)}) collective-permute-start(bf16[4,8,2048]{2,1,0:T(8,128)(2,1)S(1)} %bitcast.182), channel_id=1, source_target_pairs={{1,0},{2,1},{3,2},{4,3},{5,4},{6,5},{7,6},{8,7},{9,8},{10,9},{11,1... | collective-permute-start | bytes 393224 | tf_op jit(solution)/shard_map/while/body/eval_jaxpr/ppermute | solution.py:17
  68.4 4.4 %collective-permute-start.2 = (bf16[2,2,8,2048]{3,2,1,0:T(8,128)(2,1)S(1)}, bf16[2,2,8,2048]{3,2,1,0:T(8,128)(2,1)S(1)}, u32[]{:S(2)}, u32[]{:S(2)}) collective-permute-start(bf16[2,2,8,2048]{3,2,1,0:T(8,128)(2,1)S(1)} %fusion.119), channel_id=1, source_target_pairs={{0,16},{1,17},{2,18},{3,19},{4,20},{5,21},{6,22},{7,23},{8,24},{9,... | collective-permute-start | bytes 393224 | tf_op jit(solution)/shard_map/while/body/eval_jaxpr/ppermute | solution.py:25
  77.4 1.9 %collective-permute-start = (bf16[4,8,2048]{2,1,0:T(8,128)(2,1)S(1)}, bf16[4,8,2048]{2,1,0:T(8,128)(2,1)S(1)}, u32[]{:S(2)}, u32[]{:S(2)}) collective-permute-start(bf16[4,8,2048]{2,1,0:T(8,128)(2,1)S(1)} %bitcast.181), channel_id=1, source_target_pairs={{0,1},{1,2},{2,3},{3,4},{4,5},{5,6},{6,7},{7,8},{8,9},{9,10},{10,1... | collective-permute-start | bytes 393224 | tf_op jit(solution)/shard_map/while/body/eval_jaxpr/ppermute | solution.py:16
  79.3 4.5 %collective-permute-start.1 = (bf16[4,8,2048]{2,1,0:T(8,128)(2,1)S(1)}, bf16[4,8,2048]{2,1,0:T(8,128)(2,1)S(1)}, u32[]{:S(2)}, u32[]{:S(2)}) collective-permute-start(bf16[4,8,2048]{2,1,0:T(8,128)(2,1)S(1)} %bitcast.182), channel_id=1, source_target_pairs={{1,0},{2,1},{3,2},{4,3},{5,4},{6,5},{7,6},{8,7},{9,8},{10,9},{11,1... | collective-permute-start | bytes 393224 | tf_op jit(solution)/shard_map/while/body/eval_jaxpr/ppermute | solution.py:17
  87.3 4.4 %collective-permute-start.2 = (bf16[2,2,8,2048]{3,2,1,0:T(8,128)(2,1)S(1)}, bf16[2,2,8,2048]{3,2,1,0:T(8,128)(2,1)S(1)}, u32[]{:S(2)}, u32[]{:S(2)}) collective-permute-start(bf16[2,2,8,2048]{3,2,1,0:T(8,128)(2,1)S(1)} %fusion.119), channel_id=1, source_target_pairs={{0,16},{1,17},{2,18},{3,19},{4,20},{5,21},{6,22},{7,23},{8,24},{9,... | collective-permute-start | bytes 393224 | tf_op jit(solution)/shard_map/while/body/eval_jaxpr/ppermute | solution.py:25
  92.5 1.8 %collective-permute-done.2 = bf16[2,2,8,2048]{3,2,1,0:T(8,128)(2,1)S(1)} collective-permute-done((bf16[2,2,8,2048]{3,2,1,0:T(8,128)(2,1)S(1)}, bf16[2,2,8,2048]{3,2,1,0:T(8,128)(2,1)S(1)}, u32[]{:S(2)}, u32[]{:S(2)}) %collective-permute-start.2) | collective-permute-done | bytes 131104 | tf_op jit(solution)/shard_map/while/body/eval_jaxpr/ppermute | solution.py:25
  95.8 56.9 %while.47 = (s32[]{:T(128)}, bf16[1,2,8,2048]{3,2,1,0:T(8,128)(2,1)S(1)}, f32[1,8,2048]{2,1,0:T(8,128)S(1)}, pred[]{:T(512)}, f32[1,8,2048]{2,1,0:T(8,128)S(1)},...) while((s32[]{:T(128)}, ...), condition=%wide.region_5.6_spmd.clone, body=%wide.region_4.5_spmd.clone.sunk | while | flops 28868612 | bytes 5767526 | solution.py:181
  95.8 1.9 %collective-permute-start.3 = (bf16[2,8,2048]{2,1,0:T(8,128)(2,1)S(1)}, bf16[2,8,2048]{2,1,0:T(8,128)(2,1)S(1)}, u32[]{:S(2)}, u32[]{:S(2)}) collective-permute-start(bf16[2,8,2048]{2,1,0:T(8,128)(2,1)S(1)} %get-tuple-element.1043), channel_id=1, source_target_pairs={{0,1},{1,2},{2,3},{3,4},{4,5},{5,6},{6,7},{7,8},{8,9},{9,10},{10,1... | collective-permute-start | bytes 196616 | tf_op jit(solution)/shard_map/while/body/eval_jaxpr/ppermute | solution.py:16
  97.7 4.5 %collective-permute-start.4 = (bf16[2,8,2048]{2,1,0:T(8,128)(2,1)S(1)}, bf16[2,8,2048]{2,1,0:T(8,128)(2,1)S(1)}, u32[]{:S(2)}, u32[]{:S(2)}) collective-permute-start(bf16[2,8,2048]{2,1,0:T(8,128)(2,1)S(1)} %get-tuple-element.1043), channel_id=1, source_target_pairs={{1,0},{2,1},{3,2},{4,3},{5,4},{6,5},{7,6},{8,7},{9,8},{10,9},{11,1... | collective-permute-start | bytes 196616 | tf_op jit(solution)/shard_map/while/body/eval_jaxpr/ppermute | solution.py:17
  110.6 4.2 %collective-permute-done.5 = bf16[1,2,8,2048]{3,2,1,0:T(8,128)(2,1)S(1)} collective-permute-done((bf16[1,2,8,2048]{3,2,1,0:T(8,128)(2,1)S(1)}, bf16[1,2,8,2048]{3,2,1,0:T(8,128)(2,1)S(1)}, u32[]{:S(2)}, u32[]{:S(2)}) %collective-permute-start.5) | collective-permute-done | bytes 65568 | tf_op jit(solution)/shard_map/while/body/eval_jaxpr/ppermute | solution.py:25
  114.8 1.9 %collective-permute-start.3 = (bf16[2,8,2048]{2,1,0:T(8,128)(2,1)S(1)}, bf16[2,8,2048]{2,1,0:T(8,128)(2,1)S(1)}, u32[]{:S(2)}, u32[]{:S(2)}) collective-permute-start(bf16[2,8,2048]{2,1,0:T(8,128)(2,1)S(1)} %get-tuple-element.1043), channel_id=1, source_target_pairs={{0,1},{1,2},{2,3},{3,4},{4,5},{5,6},{6,7},{7,8},{8,9},{9,10},{10,1... | collective-permute-start | bytes 196616 | tf_op jit(solution)/shard_map/while/body/eval_jaxpr/ppermute | solution.py:16
  116.7 4.5 %collective-permute-start.4 = (bf16[2,8,2048]{2,1,0:T(8,128)(2,1)S(1)}, bf16[2,8,2048]{2,1,0:T(8,128)(2,1)S(1)}, u32[]{:S(2)}, u32[]{:S(2)}) collective-permute-start(bf16[2,8,2048]{2,1,0:T(8,128)(2,1)S(1)} %get-tuple-element.1043), channel_id=1, source_target_pairs={{1,0},{2,1},{3,2},{4,3},{5,4},{6,5},{7,6},{8,7},{9,8},{10,9},{11,1... | collective-permute-start | bytes 196616 | tf_op jit(solution)/shard_map/while/body/eval_jaxpr/ppermute | solution.py:17
  129.5 4.2 %collective-permute-done.5 = bf16[1,2,8,2048]{3,2,1,0:T(8,128)(2,1)S(1)} collective-permute-done((bf16[1,2,8,2048]{3,2,1,0:T(8,128)(2,1)S(1)}, bf16[1,2,8,2048]{3,2,1,0:T(8,128)(2,1)S(1)}, u32[]{:S(2)}, u32[]{:S(2)}) %collective-permute-start.5) | collective-permute-done | bytes 65568 | tf_op jit(solution)/shard_map/while/body/eval_jaxpr/ppermute | solution.py:25
  133.7 1.9 %collective-permute-start.3 = (bf16[2,8,2048]{2,1,0:T(8,128)(2,1)S(1)}, bf16[2,8,2048]{2,1,0:T(8,128)(2,1)S(1)}, u32[]{:S(2)}, u32[]{:S(2)}) collective-permute-start(bf16[2,8,2048]{2,1,0:T(8,128)(2,1)S(1)} %get-tuple-element.1043), channel_id=1, source_target_pairs={{0,1},{1,2},{2,3},{3,4},{4,5},{5,6},{6,7},{7,8},{8,9},{9,10},{10,1... | collective-permute-start | bytes 196616 | tf_op jit(solution)/shard_map/while/body/eval_jaxpr/ppermute | solution.py:16
  135.7 4.5 %collective-permute-start.4 = (bf16[2,8,2048]{2,1,0:T(8,128)(2,1)S(1)}, bf16[2,8,2048]{2,1,0:T(8,128)(2,1)S(1)}, u32[]{:S(2)}, u32[]{:S(2)}) collective-permute-start(bf16[2,8,2048]{2,1,0:T(8,128)(2,1)S(1)} %get-tuple-element.1043), channel_id=1, source_target_pairs={{1,0},{2,1},{3,2},{4,3},{5,4},{6,5},{7,6},{8,7},{9,8},{10,9},{11,1... | collective-permute-start | bytes 196616 | tf_op jit(solution)/shard_map/while/body/eval_jaxpr/ppermute | solution.py:17
  148.5 4.2 %collective-permute-done.5 = bf16[1,2,8,2048]{3,2,1,0:T(8,128)(2,1)S(1)} collective-permute-done((bf16[1,2,8,2048]{3,2,1,0:T(8,128)(2,1)S(1)}, bf16[1,2,8,2048]{3,2,1,0:T(8,128)(2,1)S(1)}, u32[]{:S(2)}, u32[]{:S(2)}) %collective-permute-start.5) | collective-permute-done | bytes 65568 | tf_op jit(solution)/shard_map/while/body/eval_jaxpr/ppermute | solution.py:25
  (135 shorter events, 47.5 us)
Async XLA Ops:
  7.2 30.9 %copy-start.6 = (s32[5]{0:T(128)S(1)}, s32[5]{0:T(128)}, u32[]{:S(2)}) copy-start(s32[5]{0:T(128)} %constant.467.clone.2) | copy-start | bytes 64
  7.2 30.9 %copy-start.3 = (bf16[2,2,8,2048]{3,2,1,0:T(8,128)(2,1)S(1)}, bf16[2,2,8,2048]{3,2,1,0:T(8,128)(2,1)}, u32[]{:S(2)}) copy-start(bf16[2,2,8,2048]{3,2,1,0:T(8,128)(2,1)} %param.19) | copy-start | bytes 393220
  7.2 30.9 %copy-start.4 = (bf16[2,2,8,2048]{3,2,1,0:T(8,128)(2,1)S(1)}, bf16[2,2,8,2048]{3,2,1,0:T(8,128)(2,1)}, u32[]{:S(2)}) copy-start(bf16[2,2,8,2048]{3,2,1,0:T(8,128)(2,1)} %param.20) | copy-start | bytes 393220
  7.2 30.9 %copy-start.2 = (f32[1,8,2048]{2,1,0:T(8,128)S(1)}, f32[1,8,2048]{2,1,0:T(8,128)}, u32[]{:S(2)}) copy-start(f32[1,8,2048]{2,1,0:T(8,128)} %param.22) | copy-start | bytes 196612
  7.2 30.9 %copy-start.1 = (f32[1,8,2048]{2,1,0:T(8,128)S(1)}, f32[1,8,2048]{2,1,0:T(8,128)}, u32[]{:S(2)}) copy-start(f32[1,8,2048]{2,1,0:T(8,128)} %param.23) | copy-start | bytes 196612
  7.2 30.8 %all-gather.2.cloned.1.call-start = ((), (), s32[]{:S(2)}) async-start(), calls=%async_computation | async-start | bytes 2359296 | tf_op jit(solution)/shard_map/all_gather | solution.py:118
  40.3 8.1 %collective-permute-start = (bf16[4,8,2048]{2,1,0:T(8,128)(2,1)S(1)}, bf16[4,8,2048]{2,1,0:T(8,128)(2,1)S(1)}, u32[]{:S(2)}, u32[]{:S(2)}) collective-permute-start(bf16[4,8,2048]{2,1,0:T(8,128)(2,1)S(1)} %bitcast.181), channel_id=1, source_target_pairs={{0,1},{1,2},{2,3},{3,4},{4,5},{5,6},{6,7},{7,8},{8,9},{9,10},{10,1... | collective-permute-start | bytes 393224 | tf_op jit(solution)/shard_map/while/body/eval_jaxpr/ppermute | solution.py:16
  42.2 7.0 %collective-permute-start.1 = (bf16[4,8,2048]{2,1,0:T(8,128)(2,1)S(1)}, bf16[4,8,2048]{2,1,0:T(8,128)(2,1)S(1)}, u32[]{:S(2)}, u32[]{:S(2)}) collective-permute-start(bf16[4,8,2048]{2,1,0:T(8,128)(2,1)S(1)} %bitcast.182), channel_id=1, source_target_pairs={{1,0},{2,1},{3,2},{4,3},{5,4},{6,5},{7,6},{8,7},{9,8},{10,9},{11,1... | collective-permute-start | bytes 393224 | tf_op jit(solution)/shard_map/while/body/eval_jaxpr/ppermute | solution.py:17
  50.2 6.2 %collective-permute-start.2 = (bf16[2,2,8,2048]{3,2,1,0:T(8,128)(2,1)S(1)}, bf16[2,2,8,2048]{3,2,1,0:T(8,128)(2,1)S(1)}, u32[]{:S(2)}, u32[]{:S(2)}) collective-permute-start(bf16[2,2,8,2048]{3,2,1,0:T(8,128)(2,1)S(1)} %fusion.119), channel_id=1, source_target_pairs={{0,16},{1,17},{2,18},{3,19},{4,20},{5,21},{6,22},{7,23},{8,24},{9,... | collective-permute-start | bytes 393224 | tf_op jit(solution)/shard_map/while/body/eval_jaxpr/ppermute | solution.py:25
  58.4 8.1 %collective-permute-start = (bf16[4,8,2048]{2,1,0:T(8,128)(2,1)S(1)}, bf16[4,8,2048]{2,1,0:T(8,128)(2,1)S(1)}, u32[]{:S(2)}, u32[]{:S(2)}) collective-permute-start(bf16[4,8,2048]{2,1,0:T(8,128)(2,1)S(1)} %bitcast.181), channel_id=1, source_target_pairs={{0,1},{1,2},{2,3},{3,4},{4,5},{5,6},{6,7},{7,8},{8,9},{9,10},{10,1... | collective-permute-start | bytes 393224 | tf_op jit(solution)/shard_map/while/body/eval_jaxpr/ppermute | solution.py:16
  60.4 7.0 %collective-permute-start.1 = (bf16[4,8,2048]{2,1,0:T(8,128)(2,1)S(1)}, bf16[4,8,2048]{2,1,0:T(8,128)(2,1)S(1)}, u32[]{:S(2)}, u32[]{:S(2)}) collective-permute-start(bf16[4,8,2048]{2,1,0:T(8,128)(2,1)S(1)} %bitcast.182), channel_id=1, source_target_pairs={{1,0},{2,1},{3,2},{4,3},{5,4},{6,5},{7,6},{8,7},{9,8},{10,9},{11,1... | collective-permute-start | bytes 393224 | tf_op jit(solution)/shard_map/while/body/eval_jaxpr/ppermute | solution.py:17
  68.4 6.9 %collective-permute-start.2 = (bf16[2,2,8,2048]{3,2,1,0:T(8,128)(2,1)S(1)}, bf16[2,2,8,2048]{3,2,1,0:T(8,128)(2,1)S(1)}, u32[]{:S(2)}, u32[]{:S(2)}) collective-permute-start(bf16[2,2,8,2048]{3,2,1,0:T(8,128)(2,1)S(1)} %fusion.119), channel_id=1, source_target_pairs={{0,16},{1,17},{2,18},{3,19},{4,20},{5,21},{6,22},{7,23},{8,24},{9,... | collective-permute-start | bytes 393224 | tf_op jit(solution)/shard_map/while/body/eval_jaxpr/ppermute | solution.py:25
  77.4 8.1 %collective-permute-start = (bf16[4,8,2048]{2,1,0:T(8,128)(2,1)S(1)}, bf16[4,8,2048]{2,1,0:T(8,128)(2,1)S(1)}, u32[]{:S(2)}, u32[]{:S(2)}) collective-permute-start(bf16[4,8,2048]{2,1,0:T(8,128)(2,1)S(1)} %bitcast.181), channel_id=1, source_target_pairs={{0,1},{1,2},{2,3},{3,4},{4,5},{5,6},{6,7},{7,8},{8,9},{9,10},{10,1... | collective-permute-start | bytes 393224 | tf_op jit(solution)/shard_map/while/body/eval_jaxpr/ppermute | solution.py:16
  79.3 7.0 %collective-permute-start.1 = (bf16[4,8,2048]{2,1,0:T(8,128)(2,1)S(1)}, bf16[4,8,2048]{2,1,0:T(8,128)(2,1)S(1)}, u32[]{:S(2)}, u32[]{:S(2)}) collective-permute-start(bf16[4,8,2048]{2,1,0:T(8,128)(2,1)S(1)} %bitcast.182), channel_id=1, source_target_pairs={{1,0},{2,1},{3,2},{4,3},{5,4},{6,5},{7,6},{8,7},{9,8},{10,9},{11,1... | collective-permute-start | bytes 393224 | tf_op jit(solution)/shard_map/while/body/eval_jaxpr/ppermute | solution.py:17
  87.3 6.9 %collective-permute-start.2 = (bf16[2,2,8,2048]{3,2,1,0:T(8,128)(2,1)S(1)}, bf16[2,2,8,2048]{3,2,1,0:T(8,128)(2,1)S(1)}, u32[]{:S(2)}, u32[]{:S(2)}) collective-permute-start(bf16[2,2,8,2048]{3,2,1,0:T(8,128)(2,1)S(1)} %fusion.119), channel_id=1, source_target_pairs={{0,16},{1,17},{2,18},{3,19},{4,20},{5,21},{6,22},{7,23},{8,24},{9,... | collective-permute-start | bytes 393224 | tf_op jit(solution)/shard_map/while/body/eval_jaxpr/ppermute | solution.py:25
  95.8 11.4 %collective-permute-start.3 = (bf16[2,8,2048]{2,1,0:T(8,128)(2,1)S(1)}, bf16[2,8,2048]{2,1,0:T(8,128)(2,1)S(1)}, u32[]{:S(2)}, u32[]{:S(2)}) collective-permute-start(bf16[2,8,2048]{2,1,0:T(8,128)(2,1)S(1)} %get-tuple-element.1043), channel_id=1, source_target_pairs={{0,1},{1,2},{2,3},{3,4},{4,5},{5,6},{6,7},{7,8},{8,9},{9,10},{10,1... | collective-permute-start | bytes 196616 | tf_op jit(solution)/shard_map/while/body/eval_jaxpr/ppermute | solution.py:16
  97.7 9.5 %collective-permute-start.4 = (bf16[2,8,2048]{2,1,0:T(8,128)(2,1)S(1)}, bf16[2,8,2048]{2,1,0:T(8,128)(2,1)S(1)}, u32[]{:S(2)}, u32[]{:S(2)}) collective-permute-start(bf16[2,8,2048]{2,1,0:T(8,128)(2,1)S(1)} %get-tuple-element.1043), channel_id=1, source_target_pairs={{1,0},{2,1},{3,2},{4,3},{5,4},{6,5},{7,6},{8,7},{9,8},{10,9},{11,1... | collective-permute-start | bytes 196616 | tf_op jit(solution)/shard_map/while/body/eval_jaxpr/ppermute | solution.py:17
  108.6 6.2 %collective-permute-start.5 = (bf16[1,2,8,2048]{3,2,1,0:T(8,128)(2,1)S(1)}, bf16[1,2,8,2048]{3,2,1,0:T(8,128)(2,1)S(1)}, u32[]{:S(2)}, u32[]{:S(2)}) collective-permute-start(bf16[1,2,8,2048]{3,2,1,0:T(8,128)(2,1)S(1)} %pad_maximum_fusion.11), channel_id=1, source_target_pairs={{16,0},{17,1},{18,2},{19,3},{20,4},{21,5},{22,6},{23,7},{24,8},{25... | collective-permute-start | bytes 196616 | tf_op jit(solution)/shard_map/while/body/eval_jaxpr/ppermute | solution.py:25
  114.8 11.4 %collective-permute-start.3 = (bf16[2,8,2048]{2,1,0:T(8,128)(2,1)S(1)}, bf16[2,8,2048]{2,1,0:T(8,128)(2,1)S(1)}, u32[]{:S(2)}, u32[]{:S(2)}) collective-permute-start(bf16[2,8,2048]{2,1,0:T(8,128)(2,1)S(1)} %get-tuple-element.1043), channel_id=1, source_target_pairs={{0,1},{1,2},{2,3},{3,4},{4,5},{5,6},{6,7},{7,8},{8,9},{9,10},{10,1... | collective-permute-start | bytes 196616 | tf_op jit(solution)/shard_map/while/body/eval_jaxpr/ppermute | solution.py:16
  116.7 9.5 %collective-permute-start.4 = (bf16[2,8,2048]{2,1,0:T(8,128)(2,1)S(1)}, bf16[2,8,2048]{2,1,0:T(8,128)(2,1)S(1)}, u32[]{:S(2)}, u32[]{:S(2)}) collective-permute-start(bf16[2,8,2048]{2,1,0:T(8,128)(2,1)S(1)} %get-tuple-element.1043), channel_id=1, source_target_pairs={{1,0},{2,1},{3,2},{4,3},{5,4},{6,5},{7,6},{8,7},{9,8},{10,9},{11,1... | collective-permute-start | bytes 196616 | tf_op jit(solution)/shard_map/while/body/eval_jaxpr/ppermute | solution.py:17
  127.5 6.2 %collective-permute-start.5 = (bf16[1,2,8,2048]{3,2,1,0:T(8,128)(2,1)S(1)}, bf16[1,2,8,2048]{3,2,1,0:T(8,128)(2,1)S(1)}, u32[]{:S(2)}, u32[]{:S(2)}) collective-permute-start(bf16[1,2,8,2048]{3,2,1,0:T(8,128)(2,1)S(1)} %pad_maximum_fusion.11), channel_id=1, source_target_pairs={{16,0},{17,1},{18,2},{19,3},{20,4},{21,5},{22,6},{23,7},{24,8},{25... | collective-permute-start | bytes 196616 | tf_op jit(solution)/shard_map/while/body/eval_jaxpr/ppermute | solution.py:25
  133.7 11.4 %collective-permute-start.3 = (bf16[2,8,2048]{2,1,0:T(8,128)(2,1)S(1)}, bf16[2,8,2048]{2,1,0:T(8,128)(2,1)S(1)}, u32[]{:S(2)}, u32[]{:S(2)}) collective-permute-start(bf16[2,8,2048]{2,1,0:T(8,128)(2,1)S(1)} %get-tuple-element.1043), channel_id=1, source_target_pairs={{0,1},{1,2},{2,3},{3,4},{4,5},{5,6},{6,7},{7,8},{8,9},{9,10},{10,1... | collective-permute-start | bytes 196616 | tf_op jit(solution)/shard_map/while/body/eval_jaxpr/ppermute | solution.py:16
  135.7 9.5 %collective-permute-start.4 = (bf16[2,8,2048]{2,1,0:T(8,128)(2,1)S(1)}, bf16[2,8,2048]{2,1,0:T(8,128)(2,1)S(1)}, u32[]{:S(2)}, u32[]{:S(2)}) collective-permute-start(bf16[2,8,2048]{2,1,0:T(8,128)(2,1)S(1)} %get-tuple-element.1043), channel_id=1, source_target_pairs={{1,0},{2,1},{3,2},{4,3},{5,4},{6,5},{7,6},{8,7},{9,8},{10,9},{11,1... | collective-permute-start | bytes 196616 | tf_op jit(solution)/shard_map/while/body/eval_jaxpr/ppermute | solution.py:17
  146.5 6.2 %collective-permute-start.5 = (bf16[1,2,8,2048]{3,2,1,0:T(8,128)(2,1)S(1)}, bf16[1,2,8,2048]{3,2,1,0:T(8,128)(2,1)S(1)}, u32[]{:S(2)}, u32[]{:S(2)}) collective-permute-start(bf16[1,2,8,2048]{3,2,1,0:T(8,128)(2,1)S(1)} %pad_maximum_fusion.11), channel_id=1, source_target_pairs={{16,0},{17,1},{18,2},{19,3},{20,4},{21,5},{22,6},{23,7},{24,8},{25... | collective-permute-start | bytes 196616 | tf_op jit(solution)/shard_map/while/body/eval_jaxpr/ppermute | solution.py:25
  (4 other events, 28.1 us)
Sparse Core Ops, SparseCore 0:
  9.6 28.3 all-gather.1
where the time goes:
time: 161 us; the launch traced here: 160 us
  starting transfers between devices  53.9 us (33%)
  waiting for transfers between devices  50.1 us (31%)
  other arithmetic  19.8 us (12%)
  matrix products  15.1 us (9%)
  between operations  14.2 us (9%)
  local copies, waits for them, and re-layouts  6.51 us (4%)
    all_gather x1, waiting for transfers between devices, per_device(): band = lax.all_gather(band, 'depth', axis=0, tiled=True)  28.5 us
    ppermute x6, starting transfers between devices, with_halo(): after = lax.ppermute(initial, axis, down)  27.2 us
    ppermute x6, waiting for transfers between devices, passed_along(): return lax.ppermute(block, axis, route)  18.9 us
    ppermute x6, starting transfers between devices, passed_along(): return lax.ppermute(block, axis, route)  15.1 us
    dot_general x9, matrix products, band_product_t(): jnp.einsum('acjd,jbd->acjb', tiles, band[:, offset], preferred_element_ty...  12.8 us
    ppermute x6, starting transfers between devices, with_halo(): before = lax.ppermute(last, axis, up)  11.5 us
    another operation x6, other arithmetic  4.86 us
  transfers between devices with their start and end apart: 19, of which 10 were waited for; matrix products, arithmetic and copies ran while one was open for 15% of the time, Pallas kernels for 0%

commit v1 on v0

v1 whole, which is shorter than its diff:
```python
import functools

import jax
import jax.numpy as jnp
from jax import lax
from jax.experimental import pallas as pl
from jax.experimental.pallas import tpu as pltpu
from jax.sharding import PartitionSpec as P

HALO = 8
F32 = jnp.float32
BF16 = jnp.bfloat16
WEIGHTS = [0.0] + [0.25 / k for k in range(1, HALO + 1)]
UP, DOWN, LEFT, RIGHT = range(4)


def sincos(theta):
    turns = jnp.floor(theta * 0.6366197723675814 + 0.5)
    rest = theta - turns * 1.5703125
    rest = rest - turns * 4.837512969970703125e-4
    rest = rest - turns * 7.54978995489188216e-8
    square = rest * rest
    sine = rest + rest * square * (
        -1.6666654611e-1 + square * (8.3321608736e-3 + square * -1.9515295891e-4)
    )
    cosine = (
        1.0
        - 0.5 * square
        + square
        * square
        * (
            4.166664568298827e-2
            + square * (-1.388731625493765e-3 + square * 2.443315711809948e-5)
        )
    )
    quadrant = turns.astype(jnp.int32)
    odd = (quadrant & 1) == 1
    sin_out = jnp.where(odd, cosine, sine)
    cos_out = jnp.where(odd, sine, cosine)
    sin_out = jnp.where((quadrant & 2) == 2, -sin_out, sin_out)
    cos_out = jnp.where(((quadrant + 1) & 2) == 2, -cos_out, cos_out)
    return sin_out, cos_out


def stencil(cur, prev, nxt):
    row = lax.broadcasted_iota(jnp.int32, cur.shape, 0)
    total = WEIGHTS[HALO] * (prev + nxt) - 2.0 * sum(WEIGHTS) * cur
    for k in range(1, HALO):
        inside = row >= k
        near = jnp.where(inside, WEIGHTS[k], WEIGHTS[HALO - k])
        far = jnp.where(inside, WEIGHTS[HALO - k], WEIGHTS[k])
        mixed = near * cur + far * jnp.where(inside, prev, nxt)
        total = total + pltpu.roll(mixed, HALO - k, 0)
    return total


def loop(count, body):
    if count <= 2:
        for i in range(count):
            body(i)
    else:
        lax.fori_loop(0, count, lambda i, c: (body(i), c)[1], 0)


def kernel(
    dims,
    freq_ref,
    src_ref,
    rcv_ref,
    slow_ref,
    coef_ref,
    mask_ref,
    band_ref,
    image_ref,
    grad_ref,
    fields,
    slow,
    coef,
    mask,
    band,
    band_t,
    band_edge,
    sines,
    cosines,
    phased,
    state,
    adj,
    hbuf,
    hlat,
    gbuf,
    glat,
    qbuf,
    img,
    grad,
    fsend,
    frecv,
    bsend,
    brecv,
    rsend,
    rrecv,
    esend,
    erecv,
    osend,
    orecv,
    own_sem,
    loc_sem,
):
    D, LATS, L, layers, NF, C, nb, B, W = dims
    NFC = NF // C
    me = lax.axis_index("depth")
    lat = lax.axis_index("lat")
    first = pl.multiple_of(me * W, B)
    mine = pl.ds(first, W)
    exists = {UP: lat > 0, DOWN: lat < LATS - 1, LEFT: me > 0, RIGHT: me < D - 1}
    target = {
        UP: {"lat": lat - 1},
        DOWN: {"lat": lat + 1},
        LEFT: {"depth": me - 1},
        RIGHT: {"depth": me + 1},
    }
    opposite = {UP: DOWN, DOWN: UP, LEFT: RIGHT, RIGHT: LEFT}
    DIRS = (UP, DOWN, LEFT, RIGHT)
    MESH = pl.DeviceIdType.MESH

    own_levels = pl.ds(me * layers, layers)
    local = [
        pltpu.make_async_copy(slow_ref.at[:, :, mine], slow.at[own_levels], loc_sem.at[0]),
        pltpu.make_async_copy(src_ref.at[:, :, :, mine], fields.at[0], loc_sem.at[1]),
        pltpu.make_async_copy(rcv_ref.at[:, :, :, mine], fields.at[1], loc_sem.at[2]),
        pltpu.make_async_copy(band_ref, band, loc_sem.at[3]),
        pltpu.make_async_copy(coef_ref.at[:, :, mine], coef.at[own_levels], loc_sem.at[4]),
        pltpu.make_async_copy(mask_ref.at[:, :, mine], mask.at[own_levels], loc_sem.at[5]),
    ]
    for copy in local:
        copy.start()

    barrier = pltpu.get_barrier_semaphore()
    for way in (UP, DOWN):

        @pl.when(exists[way])
        def _():
            pl.semaphore_signal(barrier, inc=1, device_id=target[way], device_id_type=MESH)

    for s in range(1, D):
        pl.semaphore_signal(
            barrier, inc=1, device_id={"depth": lax.rem(me + s, D)}, device_id_type=MESH
        )
    pl.semaphore_wait(
        barrier, (D - 1) + exists[UP].astype(jnp.int32) + exists[DOWN].astype(jnp.int32)
    )

    tables = ((slow_ref, slow), (coef_ref, coef), (mask_ref, mask))

    def table_copy(a, s):
        peer = lax.rem(me + s, D)
        return pltpu.make_async_remote_copy(
            src_ref=tables[a][0].at[:, :, pl.ds(pl.multiple_of(peer * W, B), W)],
            dst_ref=tables[a][1].at[own_levels],
            send_sem=rsend.at[a, s],
            recv_sem=rrecv.at[a, s],
            device_id={"depth": peer},
            device_id_type=MESH,
        )

    def table_wait(a, s):
        source = lax.rem(me - s + D, D)
        pltpu.make_async_remote_copy(
            src_ref=tables[a][1].at[pl.ds(source * layers, layers)],
            dst_ref=tables[a][1].at[pl.ds(source * layers, layers)],
            send_sem=rsend.at[a, s],
            recv_sem=rrecv.at[a, s],
            device_id={"depth": source},
            device_id_type=MESH,
        ).wait_recv()

    def edge_copy(way):
        j, k, slot = (0, 0, 1) if way == LEFT else (nb - 1, 2, 0)
        return pltpu.make_async_remote_copy(
            src_ref=band_ref.at[j, k],
            dst_ref=band_edge.at[slot],
            send_sem=esend.at[slot],
            recv_sem=erecv.at[slot],
            device_id=target[way],
            device_id_type=MESH,
        )

    for a in (0, 1):
        for s in range(1, D):
            table_copy(a, s).start()

    def late_sends():
        for s in range(1, D):
            table_copy(2, s).start()
        for way in (LEFT, RIGHT):

            @pl.when(exists[way])
            def _():
                edge_copy(way).start()

    def halo_copy(buf, lats, ssem, rsem, l, c, way):
        if way in (UP, DOWN):
            src = buf.at[l, c, :, pl.ds(B, W)]
            dst = lats.at[l, c, opposite[way]]
        else:
            src = buf.at[l, c, :, pl.ds(B if way == LEFT else W, B)]
            dst = buf.at[l, c, :, pl.ds(W + B if way == LEFT else 0, B)]
        return pltpu.make_async_remote_copy(
            src_ref=src,
            dst_ref=dst,
            send_sem=ssem.at[l, c, way],
            recv_sem=rsem.at[l, c, opposite[way]],
            device_id=target[way],
            device_id_type=MESH,
        )

    def send_halo(args, l, c):
        for way in DIRS:

            @pl.when(exists[way])
            def _():
                halo_copy(*args, l, c, way).start()

    def wait_halo(args, l, c, ways):
        for way in ways:

            @pl.when(exists[way])
            def _():
                halo_copy(*args, l, c, opposite[way]).wait_recv()

    forward = (hbuf, hlat, fsend, frecv)
    backward = (gbuf, glat, bsend, brecv)

    for way in (UP, DOWN):

        @pl.when(jnp.logical_not(exists[way]))
        def _():
            hlat[:, :, way] = jnp.zeros(hlat.shape[:2] + hlat.shape[3:], BF16)
            glat[:, :, way] = jnp.zeros(glat.shape[:2] + glat.shape[3:], BF16)

    for way, start, slot in ((LEFT, 0, 0), (RIGHT, W + B, 1)):

        @pl.when(jnp.logical_not(exists[way]))
        def _():
            hbuf[:, :, :, start : start + B] = jnp.zeros(hbuf.shape[:3] + (B,), BF16)
            gbuf[:, :, :, start : start + B] = jnp.zeros(gbuf.shape[:3] + (B,), BF16)
            band_edge[slot] = jnp.zeros((B, B), BF16)

    CW = min(W, 512)
    pieces = [slice(x, x + CW) for x in range(0, W, CW)]

    def omega_of(f):
        return 0.1 * (freq_ref[f].astype(F32) + 1.0)

    def angles(l):
        def one(f):
            omega = omega_of(f)
            for cols in pieces:
                sines[l, f, :, cols], cosines[l, f, :, cols] = sincos(omega * slow[l, :, cols])

        loop(NF, one)

    def store_phase(l, c, fi, s, cols, re, im):
        f = c * NFC + fi
        cosine, sine = cosines[l, f, :, cols], sines[l, f, :, cols]
        phase_re = re * cosine - im * sine
        phase_im = re * sine + im * cosine
        phased[l, f, s, 0, :, cols] = phase_re
        phased[l, f, s, 1, :, cols] = phase_im
        rows = pl.ds(pl.multiple_of((fi * 2 + s) * 16, 16), 16)
        inner = slice(cols.start + B, cols.stop + B)
        hbuf[l, c, rows, inner] = jnp.concatenate([phase_re, phase_im], axis=0).astype(BF16)

    def first_phase(c):
        def one(fi):
            f = c * NFC + fi
            for s in range(2):
                for cols in pieces:
                    re = fields[s, f, 0, :, cols].astype(F32)
                    im = fields[s, f, 1, :, cols].astype(F32)
                    store_phase(0, c, fi, s, cols, re, im)

        loop(NFC, one)

    def band_blocks(buf, matrix, l, c, blocks, rows):
        for j in blocks:
            qbuf[c, :rows, j * B : (j + 1) * B] = jnp.dot(
                buf[l, c, :, j * B : (j + 3) * B],
                matrix[j].reshape(3 * B, B),
                preferred_element_type=F32,
            )

    inner_blocks = range(1, nb - 1)
    outer_blocks = sorted({0, nb - 1})

    def lateral(buf, lats, l, c, row, cols):
        rows = pl.ds(pl.multiple_of(row, 16), 16)
        cur = buf[l, c, rows, cols.start + B : cols.stop + B].astype(F32)
        prev = lats[l, c, UP, rows, cols].astype(F32)
        nxt = lats[l, c, DOWN, rows, cols].astype(F32)
        product = qbuf[c, rows, cols]
        return [
            product[h] + stencil(cur[h], prev[h], nxt[h]) for h in (slice(0, 8), slice(8, 16))
        ]

    R, RB = NFC * 32, NFC * 16

    def forward_finish(l, c):
        wait_halo(forward, l, c, (LEFT, RIGHT))
        band_blocks(hbuf, band, l, c, outer_blocks, R)
        wait_halo(forward, l, c, (UP, DOWN))

        def one(fi):
            f = c * NFC + fi
            for cols in pieces:
                coefs = coef[l, :, cols]
                new = []
                for s in range(2):
                    q_re, q_im = lateral(hbuf, hlat, l, c, (fi * 2 + s) * 16, cols)
                    re = phased[l, f, s, 0, :, cols] - coefs * q_im
                    im = phased[l, f, s, 1, :, cols] + coefs * q_re
                    new.append((re, im))
                    if l + 1 < L:
                        store_phase(
                            l + 1,
                            c,
                            fi,
                            s,
                            cols,
                            re.astype(BF16).astype(F32),
                            im.astype(BF16).astype(F32),
                        )
                state[l, f, 0, :, cols] = new[0][0]
                state[l, f, 1, :, cols] = new[0][1]
                product = new[0][0] * new[1][0] + new[0][1] * new[1][1]
                if c == 0 and isinstance(fi, int) and fi == 0:
                    img[l, :, cols] = product
                else:
                    img[l, :, cols] += product

        if NFC > 2 and c == 0:
            img[l] = jnp.zeros(img.shape[1:], F32)
        loop(NFC, one)
        if c == C - 1:
            img[l] = img[l] * (1.0 / NF)

    results = ((img, image_ref), (grad, grad_ref))

    def own_copy(a, l):
        return pltpu.make_async_copy(
            results[a][0].at[l], results[a][1].at[l % layers, :, mine], own_sem.at[a, l % layers]
        )

    def out_copy(a, l):
        owner = l // layers
        return pltpu.make_async_remote_copy(
            src_ref=results[a][0].at[l],
            dst_ref=results[a][1].at[l % layers, :, mine],
            send_sem=osend.at[a, l],
            recv_sem=orecv.at[a, l % layers, lax.rem(owner - me + D, D)],
            device_id={"depth": owner},
            device_id_type=MESH,
        )

    def deliver(a, l):
        @pl.when(me == l // layers)
        def _():
            own_copy(a, l).start()

        @pl.when(me != l // layers)
        def _():
            out_copy(a, l).start()

    def begin_adjoint(l, c, fi, cols, mu):
        f = c * NFC + fi
        weight = mask[l, :, cols].astype(F32) * img[l, :, cols]
        coefs = coef[l, :, cols]
        scaled = []
        for part in range(2):
            value = weight * state[l, f, part, :, cols]
            if mu is not None:
                value = value + mu[part]
            adj[f, part, :, cols] = value
            scaled.append(coefs * value)
        rows = pl.ds(pl.multiple_of(fi * 16, 16), 16)
        gbuf[l, c, rows, cols.start + B : cols.stop + B] = jnp.concatenate(
            scaled, axis=0
        ).astype(BF16)

    def first_adjoint(c):
        def one(fi):
            for cols in pieces:
                begin_adjoint(L - 1, c, fi, cols, None)

        loop(NFC, one)

    def backward_finish(l, c):
        wait_halo(backward, l, c, (LEFT, RIGHT))
        band_blocks(gbuf, band_t, l, c, outer_blocks, RB)
        wait_halo(backward, l, c, (UP, DOWN))

        def one(fi):
            f = c * NFC + fi
            omega = omega_of(f)
            for cols in pieces:
                t_re, t_im = lateral(gbuf, glat, l, c, fi * 16, cols)
                back_re = adj[f, 0, :, cols] + t_im
                back_im = adj[f, 1, :, cols] - t_re
                term = omega * (
                    back_im * phased[l, f, 1, 0, :, cols] - back_re * phased[l, f, 1, 1, :, cols]
                )
                if c == 0 and isinstance(fi, int) and fi == 0:
                    grad[l, :, cols] = term
                else:
                    grad[l, :, cols] += term
                if l > 0:
                    cosine, sine = cosines[l, f, :, cols], sines[l, f, :, cols]
                    mu_re = back_re * cosine + back_im * sine
                    mu_im = back_im * cosine - back_re * sine
                    mu = [mu_re.astype(BF16).astype(F32), mu_im.astype(BF16).astype(F32)]
                    begin_adjoint(l - 1, c, fi, cols, mu)

        if NFC > 2 and c == 0:
            grad[l] = jnp.zeros(grad.shape[1:], F32)
        loop(NFC, one)
        if c == C - 1:
            grad[l] = grad[l] * (1.0 / NF)

    def arrive(a, l):
        if l % layers == 0:
            s = lax.rem(me - l // layers + D, D)

            @pl.when(s != 0)
            def _():
                table_wait(a, s)

    local[0].wait()
    arrive(0, 0)
    angles(0)
    local[1].wait()
    local[2].wait()
    for c in range(C):
        first_phase(c)
        send_halo(forward, 0, c)
    late_sends()
    local[3].wait()
    for c in range(C):
        band_blocks(hbuf, band, 0, c, inner_blocks, R)
    for l in range(1, L):
        arrive(0, l)
        angles(l)
    local[4].wait()
    arrive(1, 0)
    for l in range(L):
        if l > 0:
            arrive(1, l)
            for c in range(C):
                band_blocks(hbuf, band, l, c, inner_blocks, R)
        if l == L - 1:
            for way in (LEFT, RIGHT):

                @pl.when(exists[way])
                def _():
                    edge_copy(opposite[way]).wait_recv()

            for j in range(nb):
                parts = (
                    band_edge[0] if j == 0 else band[j - 1, 2],
                    band[j, 1],
                    band_edge[1] if j == nb - 1 else band[j + 1, 0],
                )
                for k in range(3):
                    band_t[j, k] = parts[k].astype(F32).T.astype(BF16)
        for c in range(C):
            forward_finish(l, c)
            if l + 1 < L:
                send_halo(forward, l + 1, c)
        if l + 1 < L:
            deliver(0, l)
    local[5].wait()
    for l in range(L):
        arrive(2, l)
    for c in range(C):
        first_adjoint(c)
        send_halo(backward, L - 1, c)
    deliver(0, L - 1)
    for l in reversed(range(L)):
        for c in range(C):
            band_blocks(gbuf, band_t, l, c, inner_blocks, RB)
        for c in range(C):
            backward_finish(l, c)
            if l > 0:
                send_halo(backward, l - 1, c)
        deliver(1, l)

    for l in range(L):
        for c in range(C):
            for way in DIRS:

                @pl.when(exists[way])
                def _():
                    halo_copy(*forward, l, c, way).wait_send()
                    halo_copy(*backward, l, c, way).wait_send()

    for s in range(1, D):
        for a in range(3):
            table_copy(a, s).wait_send()
    for way in (LEFT, RIGHT):

        @pl.when(exists[way])
        def _():
            edge_copy(way).wait_send()

    for a in range(2):
        for l in range(L):

            @pl.when(me == l // layers)
            def _():
                own_copy(a, l).wait()

            @pl.when(me != l // layers)
            def _():
                out_copy(a, l).wait_send()

        for i in range(layers):
            for s in range(1, D):
                source = lax.rem(me - s + D, D)
                theirs = pl.ds(pl.multiple_of(source * W, B), W)
                pltpu.make_async_remote_copy(
                    src_ref=results[a][0].at[i],
                    dst_ref=results[a][1].at[i, :, theirs],
                    send_sem=osend.at[a, i],
                    recv_sem=orecv.at[a, i, s],
                    device_id={"depth": source},
                    device_id_type=MESH,
                ).wait_recv()


def per_device(source_field, receiver_field, freq_index, slowness, ffd_coef, band, image_mask):
    D, LATS = lax.axis_size("depth"), lax.axis_size("lat")
    NF, _, height, width = source_field.shape
    layers = slowness.shape[0]
    L = layers * D
    nb, _, B, _ = band.shape
    W = width // D
    assert height == HALO and W == nb * B
    C = 2 if NF % 2 == 0 else 1
    NFC = NF // C
    dims = (D, LATS, L, layers, NF, C, nb, B, W)
    R, RB = NFC * 32, NFC * 16
    dma = pltpu.SemaphoreType.DMA
    anywhere = pl.BlockSpec(memory_space=pl.ANY)
    tile = (height, W)
    scratch = [
        pltpu.VMEM((2, NF, 2) + tile, BF16),
        pltpu.VMEM((L,) + tile, F32),
        pltpu.VMEM((L,) + tile, F32),
        pltpu.VMEM((L,) + tile, jnp.int32),
        pltpu.VMEM((nb, 3, B, B), BF16),
        pltpu.VMEM((nb, 3, B, B), BF16),
        pltpu.VMEM((2, B, B), BF16),
        pltpu.VMEM((L, NF) + tile, F32),
        pltpu.VMEM((L, NF) + tile, F32),
        pltpu.VMEM((L, NF, 2, 2) + tile, F32),
        pltpu.VMEM((L, NF, 2) + tile, F32),
        pltpu.VMEM((NF, 2) + tile, F32),
        pltpu.VMEM((L, C, R, W + 2 * B), BF16),
        pltpu.VMEM((L, C, 2, R, W), BF16),
        pltpu.VMEM((L, C, RB, W + 2 * B), BF16),
        pltpu.VMEM((L, C, 2, RB, W), BF16),
        pltpu.VMEM((C, R, W), F32),
        pltpu.VMEM((L,) + tile, F32),
        pltpu.VMEM((L,) + tile, F32),
        dma((L, C, 4)),
        dma((L, C, 4)),
        dma((L, C, 4)),
        dma((L, C, 4)),
        dma((3, D)),
        dma((3, D)),
        dma((2,)),
        dma((2,)),
        dma((2, L)),
        dma((2, layers, D)),
        dma((2, layers)),
        dma((6,)),
    ]
    return pl.pallas_call(
        functools.partial(kernel, dims),
        out_shape=[jax.ShapeDtypeStruct(slowness.shape, F32)] * 2,
        in_specs=[pl.BlockSpec(memory_space=pltpu.SMEM)] + [anywhere] * 6,
        out_specs=[anywhere] * 2,
        scratch_shapes=scratch,
        compiler_params=pltpu.CompilerParams(
            collective_id=0, has_side_effects=True, vmem_limit_bytes=48 * 1024 * 1024
        ),
    )(freq_index, source_field, receiver_field, slowness, ffd_coef, image_mask, band)


def solution(mesh):
    return jax.shard_map(
        per_device,
        mesh=mesh,
        in_specs=(
            P(None, None, "lat", None),
            P(None, None, "lat", None),
            P(),
            P("depth", "lat", None),
            P("depth", "lat", None),
            P("depth", None, None, None),
            P("depth", "lat", None),
        ),
        out_specs=(P("depth", "lat", None), P("depth", "lat", None)),
        check_vma=False,
    )
```

time: 161 us -> 32.1 us (0.20)
  starting transfers between devices: 53.9 us -> 0 us
  waiting for transfers between devices: 50.1 us -> 0 us
  Pallas kernels: 0 us -> 23.6 us
  other arithmetic: 19.8 us -> 0 us
  matrix products: 15.1 us -> 0 us
  between operations: 14.2 us -> 0.66 us
    ppermute x18 -> x0, starting transfers between devices: 53.9 us -> none  [the longest x6 27.2 us: with_halo(): after = lax.ppermute(initial, axis, down)]
    all_gather x1 -> x0, waiting for transfers between devices: 28.5 us -> none  [per_device(): band = lax.all_gather(band, 'depth', axis=0, tiled=True)]
    pallas_call x0 -> x1, Pallas kernels: none -> 23.6 us  [per_device(): pl.pallas_call(functools.partial(kernel, dims), out_shape=[jax.ShapeDtype...]
    ppermute x18 -> x0, waiting for transfers between devices: 21.6 us -> none  [the longest x6 18.9 us: passed_along(): return lax.ppermute(block, axis, route)]
    dot_general x18 -> x0, matrix products: 15.1 us -> none  [the longest x9 12.8 us: band_product_t(): jnp.einsum('acjd,jbd->acjb', tiles, band[:, offset], preferred_element_ty...]
    unnamed x13 -> x16, local copies, waits for them, and re-layouts: 2.24 us -> 7.37 us
    another operation x9 -> x0, other arithmetic: 4.89 us -> none
    add x9 -> x0, other arithmetic: 4.87 us -> none  [the longest x3 2.71 us: advance(): band_product(rows, band) + stencil_rows(rows, padded)]
  transfers between devices with their start and end apart: 19 -> 0, of which waited for: 10 -> 0; matrix products, arithmetic and copies ran while one was open for 15% -> 0% of each run, Pallas kernels for 0% -> 0%
where the time goes in v1:
time: 32.1 us; the launch traced here: 31.6 us
  Pallas kernels  23.6 us (74%)
  local copies, waits for them, and re-layouts  7.37 us (23%)
  between operations  0.66 us (2%)
    pallas_call x1, Pallas kernels, per_device(): pl.pallas_call(functools.partial(kernel, dims), out_shape=[jax.ShapeDtype...  23.6 us
    unnamed x16, local copies, waits for them, and re-layouts  7.37 us

profile of v1, /device:TPU:8, one launch (start us, length us, event | category | flops | bytes accessed | tf_op | source)
XLA Modules:
  0.0 31.6 jit_solution(11279601177191726872)
XLA Ops:
  0.6 0.0 copy-start
  0.6 1.1 %copy-done = bf16[8,3,128,128]{3,2,1,0:T(8,128)(2,1)S(1)} copy-done((bf16[8,3,128,128]{3,2,1,0:T(8,128)(2,1)S(1)}, bf16[8,3,128,128]{3,2,1,0:T(8,128)(2,1)}, u32[]{:S(2)}) %copy-start) | copy-done | bytes 786456
  1.8 0.0 copy-start.1
  1.8 0.9 %copy-done.1 = bf16[2,2,8,2048]{3,2,1,0:T(8,128)(2,1)S(1)} copy-done((bf16[2,2,8,2048]{3,2,1,0:T(8,128)(2,1)S(1)}, bf16[2,2,8,2048]{3,2,1,0:T(8,128)(2,1)}, u32[]{:S(2)}) %copy-start.1) | copy-done | bytes 131096
  2.7 0.0 copy-start.2
  2.7 0.9 %copy-done.2 = bf16[2,2,8,2048]{3,2,1,0:T(8,128)(2,1)S(1)} copy-done((bf16[2,2,8,2048]{3,2,1,0:T(8,128)(2,1)S(1)}, bf16[2,2,8,2048]{3,2,1,0:T(8,128)(2,1)}, u32[]{:S(2)}) %copy-start.2) | copy-done | bytes 131096
  3.6 0.0 copy-start.3
  3.6 0.8 %copy-done.3 = f32[1,8,2048]{2,1,0:T(8,128)S(1)} copy-done((f32[1,8,2048]{2,1,0:T(8,128)S(1)}, f32[1,8,2048]{2,1,0:T(8,128)}, u32[]{:S(2)}) %copy-start.3) | copy-done | bytes 65560
  4.4 0.0 copy-start.4
  4.4 0.8 %copy-done.4 = f32[1,8,2048]{2,1,0:T(8,128)S(1)} copy-done((f32[1,8,2048]{2,1,0:T(8,128)S(1)}, f32[1,8,2048]{2,1,0:T(8,128)}, u32[]{:S(2)}) %copy-start.4) | copy-done | bytes 65560
  5.3 0.0 copy-start.5
  5.3 0.8 %copy-done.5 = s32[1,8,2048]{2,1,0:T(8,128)S(1)} copy-done((s32[1,8,2048]{2,1,0:T(8,128)S(1)}, s32[1,8,2048]{2,1,0:T(8,128)}, u32[]{:S(2)}) %copy-start.5) | copy-done | bytes 65560
  6.1 0.0 copy-start.6
  6.1 0.7 %copy-done.6 = s32[2]{0:T(128)S(1)} copy-done((s32[2]{0:T(128)S(1)}, s32[2]{0:T(128)}, u32[]{:S(2)}) %copy-start.6) | copy-done | bytes 32
  6.8 23.6 %shard_map.86 = (f32[1,8,2048]{2,1,0:T(8,128)S(1)}, f32[1,8,2048]{2,1,0:T(8,128)S(1)}) custom-call(s32[2]{0:T(128)S(1)} %copy-done.6, bf16[2,2,8,2048]{3,2,1,0:T(8,128)(2,1)S(1)} %copy-done.1, bf16[2,2,8,2048]{3,2,1,0:T(8,128)(2,1)S(1)} %copy-done.2, f32[1,8,2048]{2,1,0:T(8,128)S(1)} %copy-done.3, f32[1,8,2048]{2,1,0:T(8,128)S(1)} %copy-done.4, ...), custom_call_target="tpu_custom_call" | custom-call | tf_op jit(solution)/shard_map/pallas_call | solution.py:586
  30.4 0.6 %copy.11 = f32[1,8,2048]{2,1,0:T(8,128)} copy(f32[1,8,2048]{2,1,0:T(8,128)S(1)} %get-tuple-element.4) | data formatting | bytes 131072
  31.0 0.6 %copy.12 = f32[1,8,2048]{2,1,0:T(8,128)} copy(f32[1,8,2048]{2,1,0:T(8,128)S(1)} %get-tuple-element.5) | data formatting | bytes 131072
Async XLA Ops:
  0.6 1.1 %copy-start = (bf16[8,3,128,128]{3,2,1,0:T(8,128)(2,1)S(1)}, bf16[8,3,128,128]{3,2,1,0:T(8,128)(2,1)}, u32[]{:S(2)}) copy-start(bf16[8,3,128,128]{3,2,1,0:T(8,128)(2,1)} %band_ref.1) | copy-start | bytes 2359300
  1.8 0.9 %copy-start.1 = (bf16[2,2,8,2048]{3,2,1,0:T(8,128)(2,1)S(1)}, bf16[2,2,8,2048]{3,2,1,0:T(8,128)(2,1)}, u32[]{:S(2)}) copy-start(bf16[2,2,8,2048]{3,2,1,0:T(8,128)(2,1)} %src_ref.1) | copy-start | bytes 393220
  2.7 0.9 %copy-start.2 = (bf16[2,2,8,2048]{3,2,1,0:T(8,128)(2,1)S(1)}, bf16[2,2,8,2048]{3,2,1,0:T(8,128)(2,1)}, u32[]{:S(2)}) copy-start(bf16[2,2,8,2048]{3,2,1,0:T(8,128)(2,1)} %rcv_ref.1) | copy-start | bytes 393220
  3.6 0.8 %copy-start.3 = (f32[1,8,2048]{2,1,0:T(8,128)S(1)}, f32[1,8,2048]{2,1,0:T(8,128)}, u32[]{:S(2)}) copy-start(f32[1,8,2048]{2,1,0:T(8,128)} %slow_ref.1) | copy-start | bytes 196612
  4.4 0.8 %copy-start.4 = (f32[1,8,2048]{2,1,0:T(8,128)S(1)}, f32[1,8,2048]{2,1,0:T(8,128)}, u32[]{:S(2)}) copy-start(f32[1,8,2048]{2,1,0:T(8,128)} %coef_ref.1) | copy-start | bytes 196612
  5.3 0.8 %copy-start.5 = (s32[1,8,2048]{2,1,0:T(8,128)S(1)}, s32[1,8,2048]{2,1,0:T(8,128)}, u32[]{:S(2)}) copy-start(s32[1,8,2048]{2,1,0:T(8,128)} %mask_ref.1) | copy-start | bytes 196612
  6.1 0.7 %copy-start.6 = (s32[2]{0:T(128)S(1)}, s32[2]{0:T(128)}, u32[]{:S(2)}) copy-start(s32[2]{0:T(128)} %freq_ref.1) | copy-start | bytes 28

commit v2 on v1

--- a/solution.py
+++ b/solution.py
@@ -64,7 +64,7 @@
 
 def kernel(
     dims,
-    freq_ref,
+    freq_hbm,
     src_ref,
     rcv_ref,
     slow_ref,
@@ -73,6 +73,7 @@
     band_ref,
     image_ref,
     grad_ref,
+    freq_ref,
     fields,
     slow,
     coef,
@@ -104,8 +105,9 @@
     orecv,
     own_sem,
     loc_sem,
+    band_sem,
 ):
-    D, LATS, L, layers, NF, C, nb, B, W = dims
+    D, LATS, L, layers, NF, C, nb, G, B, W = dims
     NFC = NF // C
     me = lax.axis_index("depth")
     lat = lax.axis_index("lat")
@@ -119,7 +121,7 @@
         RIGHT: {"depth": me + 1},
     }
     opposite = {UP: DOWN, DOWN: UP, LEFT: RIGHT, RIGHT: LEFT}
-    DIRS = (UP, DOWN, LEFT, RIGHT)
+    DIRS = (LEFT, RIGHT, UP, DOWN)
     MESH = pl.DeviceIdType.MESH
 
     own_levels = pl.ds(me * layers, layers)
@@ -127,9 +129,14 @@
         pltpu.make_async_copy(slow_ref.at[:, :, mine], slow.at[own_levels], loc_sem.at[0]),
         pltpu.make_async_copy(src_ref.at[:, :, :, mine], fields.at[0], loc_sem.at[1]),
         pltpu.make_async_copy(rcv_ref.at[:, :, :, mine], fields.at[1], loc_sem.at[2]),
-        pltpu.make_async_copy(band_ref, band, loc_sem.at[3]),
-        pltpu.make_async_copy(coef_ref.at[:, :, mine], coef.at[own_levels], loc_sem.at[4]),
-        pltpu.make_async_copy(mask_ref.at[:, :, mine], mask.at[own_levels], loc_sem.at[5]),
+        pltpu.make_async_copy(coef_ref.at[:, :, mine], coef.at[own_levels], loc_sem.at[3]),
+        pltpu.make_async_copy(mask_ref.at[:, :, mine], mask.at[own_levels], loc_sem.at[4]),
+        pltpu.make_async_copy(freq_hbm, freq_ref, loc_sem.at[5]),
+    ] + [
+        pltpu.make_async_copy(
+            band_ref.at[:, e], band.at[:, e : e + 3, :, e * B : (e + 1) * B], band_sem.at[e]
+        )
+        for e in range(G)
     ]
     for copy in local:
         copy.start()
@@ -145,6 +152,27 @@
         pl.semaphore_signal(
             barrier, inc=1, device_id={"depth": lax.rem(me + s, D)}, device_id_type=MESH
         )
+    for way in (UP, DOWN):
+
+        @pl.when(jnp.logical_not(exists[way]))
+        def _():
+            hlat[:, :, way] = jnp.zeros(hlat.shape[:2] + hlat.shape[3:], BF16)
+            glat[:, :, way] = jnp.zeros(glat.shape[:2] + glat.shape[3:], BF16)
+
+    for way, start, slot in ((LEFT, 0, 0), (RIGHT, W + B, 1)):
+
+        @pl.when(jnp.logical_not(exists[way]))
+        def _():
+            hbuf[:, :, :, start : start + B] = jnp.zeros(hbuf.shape[:3] + (B,), BF16)
+            gbuf[:, :, :, start : start + B] = jnp.zeros(gbuf.shape[:3] + (B,), BF16)
+            band_edge[slot] = jnp.zeros((B, B), BF16)
+
+    for matrix in (band, band_t):
+        for e in range(G):
+            for r in range(G + 2):
+                if not e <= r < e + 3:
+                    matrix[:, r, :, e * B : (e + 1) * B] = jnp.zeros((nb // G, B, B), BF16)
+
     pl.semaphore_wait(
         barrier, (D - 1) + exists[UP].astype(jnp.int32) + exists[DOWN].astype(jnp.int32)
     )
@@ -176,7 +204,7 @@
     def edge_copy(way):
         j, k, slot = (0, 0, 1) if way == LEFT else (nb - 1, 2, 0)
         return pltpu.make_async_remote_copy(
-            src_ref=band_ref.at[j, k],
+            src_ref=band_ref.at[j // G, j % G, k],
             dst_ref=band_edge.at[slot],
             send_sem=esend.at[slot],
             recv_sem=erecv.at[slot],
@@ -230,21 +258,6 @@
     forward = (hbuf, hlat, fsend, frecv)
     backward = (gbuf, glat, bsend, brecv)
 
-    for way in (UP, DOWN):
-
-        @pl.when(jnp.logical_not(exists[way]))
-        def _():
-            hlat[:, :, way] = jnp.zeros(hlat.shape[:2] + hlat.shape[3:], BF16)
-            glat[:, :, way] = jnp.zeros(glat.shape[:2] + glat.shape[3:], BF16)
-
-    for way, start, slot in ((LEFT, 0, 0), (RIGHT, W + B, 1)):
-
-        @pl.when(jnp.logical_not(exists[way]))
-        def _():
-            hbuf[:, :, :, start : start + B] = jnp.zeros(hbuf.shape[:3] + (B,), BF16)
-            gbuf[:, :, :, start : start + B] = jnp.zeros(gbuf.shape[:3] + (B,), BF16)
-            band_edge[slot] = jnp.zeros((B, B), BF16)
-
     CW = min(W, 512)
     pieces = [slice(x, x + CW) for x in range(0, W, CW)]
 
@@ -281,32 +294,37 @@
 
         loop(NFC, one)
 
-    def band_blocks(buf, matrix, l, c, blocks, rows):
-        for j in blocks:
-            qbuf[c, :rows, j * B : (j + 1) * B] = jnp.dot(
-                buf[l, c, :, j * B : (j + 3) * B],
-                matrix[j].reshape(3 * B, B),
+    R, RB = NFC * 32, NFC * 16
+
+    def band_groups(buf, matrix, l, groups, rows):
+        for p in groups:
+            left = p * G * B
+            qbuf[: C * rows, left : left + G * B] = jnp.dot(
+                buf[l, :, :, left : left + (G + 2) * B].reshape(C * rows, (G + 2) * B),
+                matrix[p].reshape((G + 2) * B, G * B),
                 preferred_element_type=F32,
             )
 
-    inner_blocks = range(1, nb - 1)
-    outer_blocks = sorted({0, nb - 1})
+    inner_groups = range(1, nb // G - 1)
+    outer_groups = sorted({0, nb // G - 1})
+
+    def band_products(args, matrix, l, rows):
+        band_groups(args[0], matrix, l, inner_groups, rows)
+        for c in range(C):
+            wait_halo(args, l, c, (LEFT, RIGHT))
+        band_groups(args[0], matrix, l, outer_groups, rows)
 
     def lateral(buf, lats, l, c, row, cols):
         rows = pl.ds(pl.multiple_of(row, 16), 16)
         cur = buf[l, c, rows, cols.start + B : cols.stop + B].astype(F32)
         prev = lats[l, c, UP, rows, cols].astype(F32)
         nxt = lats[l, c, DOWN, rows, cols].astype(F32)
-        product = qbuf[c, rows, cols]
+        product = qbuf[pl.ds(pl.multiple_of(c * buf.shape[2] + row, 16), 16), cols]
         return [
             product[h] + stencil(cur[h], prev[h], nxt[h]) for h in (slice(0, 8), slice(8, 16))
         ]
 
-    R, RB = NFC * 32, NFC * 16
-
     def forward_finish(l, c):
-        wait_halo(forward, l, c, (LEFT, RIGHT))
-        band_blocks(hbuf, band, l, c, outer_blocks, R)
         wait_halo(forward, l, c, (UP, DOWN))
 
         def one(fi):
@@ -394,8 +412,6 @@
         loop(NFC, one)
 
     def backward_finish(l, c):
-        wait_halo(backward, l, c, (LEFT, RIGHT))
-        band_blocks(gbuf, band_t, l, c, outer_blocks, RB)
         wait_halo(backward, l, c, (UP, DOWN))
 
         def one(fi):
@@ -433,7 +449,24 @@
             def _():
                 table_wait(a, s)
 
+    def transpose(j, k):
+        i = j + k - 1
+        if k != 1 and not 0 <= j < nb:
+            value = band_edge[0 if j < 0 else 1]
+        else:
+            value = band[j // G, j % G + k, :, (j % G) * B : (j % G + 1) * B]
+        band_t[i // G, i % G + 2 - k, :, (i % G) * B : (i % G + 1) * B] = (
+            value.astype(F32).T.astype(BF16)
+        )
+
+    for copy in local[6:]:
+        copy.wait()
+    for j in range(nb):
+        for k in range(3):
+            if 0 <= j + k - 1 < nb:
+                transpose(j, k)
     local[0].wait()
+    local[5].wait()
     arrive(0, 0)
     angles(0)
     local[1].wait()
@@ -442,19 +475,15 @@
         first_phase(c)
         send_halo(forward, 0, c)
     late_sends()
-    local[3].wait()
-    for c in range(C):
-        band_blocks(hbuf, band, 0, c, inner_blocks, R)
     for l in range(1, L):
         arrive(0, l)
         angles(l)
-    local[4].wait()
+    local[3].wait()
     arrive(1, 0)
     for l in range(L):
         if l > 0:
             arrive(1, l)
-            for c in range(C):
-                band_blocks(hbuf, band, l, c, inner_blocks, R)
+        band_products(forward, band, l, R)
         if l == L - 1:
             for way in (LEFT, RIGHT):
 
@@ -462,21 +491,15 @@
                 def _():
                     edge_copy(opposite[way]).wait_recv()
 
-            for j in range(nb):
-                parts = (
-                    band_edge[0] if j == 0 else band[j - 1, 2],
-                    band[j, 1],
-                    band_edge[1] if j == nb - 1 else band[j + 1, 0],
-                )
-                for k in range(3):
-                    band_t[j, k] = parts[k].astype(F32).T.astype(BF16)
+            transpose(-1, 2)
+            transpose(nb, 0)
         for c in range(C):
             forward_finish(l, c)
             if l + 1 < L:
                 send_halo(forward, l + 1, c)
         if l + 1 < L:
             deliver(0, l)
-    local[5].wait()
+    local[4].wait()
     for l in range(L):
         arrive(2, l)
     for c in range(C):
@@ -484,8 +507,7 @@
         send_halo(backward, L - 1, c)
     deliver(0, L - 1)
     for l in reversed(range(L)):
-        for c in range(C):
-            band_blocks(gbuf, band_t, l, c, inner_blocks, RB)
+        band_products(backward, band_t, l, RB)
         for c in range(C):
             backward_finish(l, c)
             if l > 0:
@@ -545,18 +567,21 @@
     assert height == HALO and W == nb * B
     C = 2 if NF % 2 == 0 else 1
     NFC = NF // C
-    dims = (D, LATS, L, layers, NF, C, nb, B, W)
+    G = 2 if nb % 2 == 0 else 1
+    dims = (D, LATS, L, layers, NF, C, nb, G, B, W)
     R, RB = NFC * 32, NFC * 16
     dma = pltpu.SemaphoreType.DMA
     anywhere = pl.BlockSpec(memory_space=pl.ANY)
+    in_hbm = pl.BlockSpec(memory_space=pltpu.HBM)
     tile = (height, W)
     scratch = [
+        pltpu.SMEM((NF,), jnp.int32),
         pltpu.VMEM((2, NF, 2) + tile, BF16),
         pltpu.VMEM((L,) + tile, F32),
         pltpu.VMEM((L,) + tile, F32),
         pltpu.VMEM((L,) + tile, jnp.int32),
-        pltpu.VMEM((nb, 3, B, B), BF16),
-        pltpu.VMEM((nb, 3, B, B), BF16),
+        pltpu.VMEM((nb // G, G + 2, B, G * B), BF16),
+        pltpu.VMEM((nb // G, G + 2, B, G * B), BF16),
         pltpu.VMEM((2, B, B), BF16),
         pltpu.VMEM((L, NF) + tile, F32),
         pltpu.VMEM((L, NF) + tile, F32),
@@ -567,7 +592,7 @@
         pltpu.VMEM((L, C, 2, R, W), BF16),
         pltpu.VMEM((L, C, RB, W + 2 * B), BF16),
         pltpu.VMEM((L, C, 2, RB, W), BF16),
-        pltpu.VMEM((C, R, W), F32),
+        pltpu.VMEM((C * R, W), F32),
         pltpu.VMEM((L,) + tile, F32),
         pltpu.VMEM((L,) + tile, F32),
         dma((L, C, 4)),
@@ -582,17 +607,18 @@
         dma((2, layers, D)),
         dma((2, layers)),
         dma((6,)),
+        dma((G,)),
     ]
     return pl.pallas_call(
         functools.partial(kernel, dims),
         out_shape=[jax.ShapeDtypeStruct(slowness.shape, F32)] * 2,
-        in_specs=[pl.BlockSpec(memory_space=pltpu.SMEM)] + [anywhere] * 6,
+        in_specs=[in_hbm] * 7,
         out_specs=[anywhere] * 2,
         scratch_shapes=scratch,
         compiler_params=pltpu.CompilerParams(
             collective_id=0, has_side_effects=True, vmem_limit_bytes=48 * 1024 * 1024
         ),
-    )(freq_index, source_field, receiver_field, slowness, ffd_coef, image_mask, band)
+    )(freq_index, source_field, receiver_field, slowness, ffd_coef, image_mask, band.reshape(nb // G, G, 3, B, B))
 
 
 def solution(mesh):

time: 32.1 us -> 31.8 us (level)
  Pallas kernels: 23.6 us -> 23.2 us
    pallas_call x1, Pallas kernels: 23.6 us -> 23.2 us  [per_device(): pl.pallas_call(functools.partial(kernel, dims), out_shape=[jax.ShapeDtype...]
where the time goes in v2:
time: 31.8 us; the launch traced here: 31.2 us
  Pallas kernels  23.2 us (73%)
  local copies, waits for them, and re-layouts  7.37 us (23%)
  between operations  0.66 us (2%)
    pallas_call x1, Pallas kernels, per_device(): pl.pallas_call(functools.partial(kernel, dims), out_shape=[jax.ShapeDtype...  23.2 us
    unnamed x16, local copies, waits for them, and re-layouts  7.37 us

profile of v2, /device:TPU:8, one launch (start us, length us, event | category | flops | bytes accessed | tf_op | source)
XLA Modules:
  0.0 31.2 jit_solution(10134530395252413260)
XLA Ops:
  0.6 0.0 copy-start.6
  0.6 0.6 %copy-done.6 = s32[2]{0:T(128)S(1)} copy-done((s32[2]{0:T(128)S(1)}, s32[2]{0:T(128)}, u32[]{:S(2)}) %copy-start.6) | copy-done | bytes 32
  1.3 0.0 copy-start
  1.3 1.1 %copy-done = bf16[8,3,128,128]{3,2,1,0:T(8,128)(2,1)S(1)} copy-done((bf16[8,3,128,128]{3,2,1,0:T(8,128)(2,1)S(1)}, bf16[8,3,128,128]{3,2,1,0:T(8,128)(2,1)}, u32[]{:S(2)}) %copy-start) | copy-done | bytes 786456
  2.4 0.0 copy-start.1
  2.4 0.9 %copy-done.1 = bf16[2,2,8,2048]{3,2,1,0:T(8,128)(2,1)S(1)} copy-done((bf16[2,2,8,2048]{3,2,1,0:T(8,128)(2,1)S(1)}, bf16[2,2,8,2048]{3,2,1,0:T(8,128)(2,1)}, u32[]{:S(2)}) %copy-start.1) | copy-done | bytes 131096
  3.3 0.0 copy-start.2
  3.3 0.9 %copy-done.2 = bf16[2,2,8,2048]{3,2,1,0:T(8,128)(2,1)S(1)} copy-done((bf16[2,2,8,2048]{3,2,1,0:T(8,128)(2,1)S(1)}, bf16[2,2,8,2048]{3,2,1,0:T(8,128)(2,1)}, u32[]{:S(2)}) %copy-start.2) | copy-done | bytes 131096
  4.2 0.0 copy-start.3
  4.2 0.8 %copy-done.3 = f32[1,8,2048]{2,1,0:T(8,128)S(1)} copy-done((f32[1,8,2048]{2,1,0:T(8,128)S(1)}, f32[1,8,2048]{2,1,0:T(8,128)}, u32[]{:S(2)}) %copy-start.3) | copy-done | bytes 65560
  5.1 0.0 copy-start.4
  5.1 0.8 %copy-done.4 = f32[1,8,2048]{2,1,0:T(8,128)S(1)} copy-done((f32[1,8,2048]{2,1,0:T(8,128)S(1)}, f32[1,8,2048]{2,1,0:T(8,128)}, u32[]{:S(2)}) %copy-start.4) | copy-done | bytes 65560
  5.9 0.0 copy-start.5
  5.9 0.8 %copy-done.5 = s32[1,8,2048]{2,1,0:T(8,128)S(1)} copy-done((s32[1,8,2048]{2,1,0:T(8,128)S(1)}, s32[1,8,2048]{2,1,0:T(8,128)}, u32[]{:S(2)}) %copy-start.5) | copy-done | bytes 65560
  6.8 23.2 %shard_map.86 = (f32[1,8,2048]{2,1,0:T(8,128)S(1)}, f32[1,8,2048]{2,1,0:T(8,128)S(1)}) custom-call(s32[2]{0:T(128)S(1)} %copy-done.6, bf16[2,2,8,2048]{3,2,1,0:T(8,128)(2,1)S(1)} %copy-done.1, bf16[2,2,8,2048]{3,2,1,0:T(8,128)(2,1)S(1)} %copy-done.2, f32[1,8,2048]{2,1,0:T(8,128)S(1)} %copy-done.3, f32[1,8,2048]{2,1,0:T(8,128)S(1)} %copy-done.4, ...), custom_call_target="tpu_custom_call" | custom-call | tf_op jit(solution)/shard_map/pallas_call | solution.py:612
  29.9 0.6 %copy.11 = f32[1,8,2048]{2,1,0:T(8,128)} copy(f32[1,8,2048]{2,1,0:T(8,128)S(1)} %get-tuple-element.4) | data formatting | bytes 131072
  30.6 0.6 %copy.12 = f32[1,8,2048]{2,1,0:T(8,128)} copy(f32[1,8,2048]{2,1,0:T(8,128)S(1)} %get-tuple-element.5) | data formatting | bytes 131072
Async XLA Ops:
  0.6 0.7 %copy-start.6 = (s32[2]{0:T(128)S(1)}, s32[2]{0:T(128)}, u32[]{:S(2)}) copy-start(s32[2]{0:T(128)} %freq_hbm.1) | copy-start | bytes 28
  1.3 1.1 %copy-start = (bf16[8,3,128,128]{3,2,1,0:T(8,128)(2,1)S(1)}, bf16[8,3,128,128]{3,2,1,0:T(8,128)(2,1)}, u32[]{:S(2)}) copy-start(bf16[8,3,128,128]{3,2,1,0:T(8,128)(2,1)} %param.12) | copy-start | bytes 2359300
  2.4 0.9 %copy-start.1 = (bf16[2,2,8,2048]{3,2,1,0:T(8,128)(2,1)S(1)}, bf16[2,2,8,2048]{3,2,1,0:T(8,128)(2,1)}, u32[]{:S(2)}) copy-start(bf16[2,2,8,2048]{3,2,1,0:T(8,128)(2,1)} %src_ref.1) | copy-start | bytes 393220
  3.3 0.9 %copy-start.2 = (bf16[2,2,8,2048]{3,2,1,0:T(8,128)(2,1)S(1)}, bf16[2,2,8,2048]{3,2,1,0:T(8,128)(2,1)}, u32[]{:S(2)}) copy-start(bf16[2,2,8,2048]{3,2,1,0:T(8,128)(2,1)} %rcv_ref.1) | copy-start | bytes 393220
  4.2 0.8 %copy-start.3 = (f32[1,8,2048]{2,1,0:T(8,128)S(1)}, f32[1,8,2048]{2,1,0:T(8,128)}, u32[]{:S(2)}) copy-start(f32[1,8,2048]{2,1,0:T(8,128)} %slow_ref.1) | copy-start | bytes 196612
  5.1 0.8 %copy-start.4 = (f32[1,8,2048]{2,1,0:T(8,128)S(1)}, f32[1,8,2048]{2,1,0:T(8,128)}, u32[]{:S(2)}) copy-start(f32[1,8,2048]{2,1,0:T(8,128)} %coef_ref.1) | copy-start | bytes 196612
  5.9 0.8 %copy-start.5 = (s32[1,8,2048]{2,1,0:T(8,128)S(1)}, s32[1,8,2048]{2,1,0:T(8,128)}, u32[]{:S(2)}) copy-start(s32[1,8,2048]{2,1,0:T(8,128)} %mask_ref.1) | copy-start | bytes 196612

commit v3 on v2

--- a/solution.py
+++ b/solution.py
@@ -8,6 +8,7 @@
 from jax.sharding import PartitionSpec as P
 
 HALO = 8
+VMEM_BYTES = 64 * 1024 * 1024
 F32 = jnp.float32
 BF16 = jnp.bfloat16
 WEIGHTS = [0.0] + [0.25 / k for k in range(1, HALO + 1)]
@@ -557,6 +558,17 @@
                 ).wait_recv()
 
 
+def publish(image_in, grad_in, image_out, grad_out, sems):
+    copies = [
+        pltpu.make_async_copy(image_in, image_out, sems.at[0]),
+        pltpu.make_async_copy(grad_in, grad_out, sems.at[1]),
+    ]
+    for copy in copies:
+        copy.start()
+    for copy in copies:
+        copy.wait()
+
+
 def per_device(source_field, receiver_field, freq_index, slowness, ffd_coef, band, image_mask):
     D, LATS = lax.axis_size("depth"), lax.axis_size("lat")
     NF, _, height, width = source_field.shape
@@ -571,7 +583,6 @@
     dims = (D, LATS, L, layers, NF, C, nb, G, B, W)
     R, RB = NFC * 32, NFC * 16
     dma = pltpu.SemaphoreType.DMA
-    anywhere = pl.BlockSpec(memory_space=pl.ANY)
     in_hbm = pl.BlockSpec(memory_space=pltpu.HBM)
     tile = (height, W)
     scratch = [
@@ -609,16 +620,24 @@
         dma((6,)),
         dma((G,)),
     ]
-    return pl.pallas_call(
+    image, grad = pl.pallas_call(
         functools.partial(kernel, dims),
         out_shape=[jax.ShapeDtypeStruct(slowness.shape, F32)] * 2,
         in_specs=[in_hbm] * 7,
-        out_specs=[anywhere] * 2,
+        out_specs=[in_hbm] * 2,
         scratch_shapes=scratch,
         compiler_params=pltpu.CompilerParams(
-            collective_id=0, has_side_effects=True, vmem_limit_bytes=48 * 1024 * 1024
+            collective_id=0, has_side_effects=True, vmem_limit_bytes=VMEM_BYTES
         ),
     )(freq_index, source_field, receiver_field, slowness, ffd_coef, image_mask, band.reshape(nb // G, G, 3, B, B))
+    return pl.pallas_call(
+        publish,
+        out_shape=[jax.ShapeDtypeStruct(slowness.shape, F32)] * 2,
+        in_specs=[in_hbm] * 2,
+        out_specs=[in_hbm] * 2,
+        scratch_shapes=[dma((2,))],
+        compiler_params=pltpu.CompilerParams(vmem_limit_bytes=VMEM_BYTES),
+    )(image, grad)
 
 
 def solution(mesh):

time: 31.8 us -> 29.4 us (0.925)
  local copies, waits for them, and re-layouts: 7.37 us -> 0 us
  Pallas kernels: 23.2 us -> 28.4 us
    unnamed x16 -> x0, local copies, waits for them, and re-layouts: 7.37 us -> none
    pallas_call x0 -> x1, Pallas kernels: none -> 5.09 us  [per_device(): pl.pallas_call(publish, out_shape=[jax.ShapeDtypeStruct(slowness.shape, F...]
where the time goes in v3:
time: 29.4 us; the launch traced here: 29 us
  Pallas kernels  28.4 us (97%)
  between operations  0.64 us (2%)
    pallas_call x1, Pallas kernels, per_device(): pl.pallas_call(functools.partial(kernel, dims), out_shape=[jax.ShapeDtype...  23.3 us
    pallas_call x1, Pallas kernels, per_device(): pl.pallas_call(publish, out_shape=[jax.ShapeDtypeStruct(slowness.shape, F...  5.09 us

profile of v3, /device:TPU:8, one launch (start us, length us, event | category | flops | bytes accessed | tf_op | source)
XLA Modules:
  0.0 29.0 jit_solution(8574122227511017838)
XLA Ops:
  0.6 23.3 %shard_map.86 = (f32[1,8,2048]{2,1,0:T(8,128)}, f32[1,8,2048]{2,1,0:T(8,128)}) custom-call(s32[2]{0:T(128)} %freq_hbm.1, bf16[2,2,8,2048]{3,2,1,0:T(8,128)(2,1)} %src_ref.1, bf16[2,2,8,2048]{3,2,1,0:T(8,128)(2,1)} %rcv_ref.1, f32[1,8,2048]{2,1,0:T(8,128)} %slow_ref.1, f32[1,8,2048]{2,1,0:T(8,128)} %coef_ref.1, s32[1,8,2048]{2,1,0:T(8,128)} %mask_ref.1, ...), custom_call_target="tpu_custom_call" | custom-call | tf_op jit(solution)/shard_map/pallas_call | solution.py:623
  23.9 5.1 %shard_map.87 = (f32[1,8,2048]{2,1,0:T(8,128)}, f32[1,8,2048]{2,1,0:T(8,128)}) custom-call(f32[1,8,2048]{2,1,0:T(8,128)} %get-tuple-element.4.image_in, f32[1,8,2048]{2,1,0:T(8,128)} %get-tuple-element.5.grad_in), custom_call_target="tpu_custom_call" | custom-call | tf_op jit(solution)/shard_map/pallas_call | solution.py:633

commit v4 on v3

--- a/solution.py
+++ b/solution.py
@@ -8,7 +8,7 @@
 from jax.sharding import PartitionSpec as P
 
 HALO = 8
-VMEM_BYTES = 64 * 1024 * 1024
+VMEM_BYTES = 64 * 1024 * 1024 - 208 * 1024
 F32 = jnp.float32
 BF16 = jnp.bfloat16
 WEIGHTS = [0.0] + [0.25 / k for k in range(1, HALO + 1)]
@@ -583,6 +583,7 @@
     dims = (D, LATS, L, layers, NF, C, nb, G, B, W)
     R, RB = NFC * 32, NFC * 16
     dma = pltpu.SemaphoreType.DMA
+    anywhere = pl.BlockSpec(memory_space=pl.ANY)
     in_hbm = pl.BlockSpec(memory_space=pltpu.HBM)
     tile = (height, W)
     scratch = [
@@ -622,9 +623,9 @@
     ]
     image, grad = pl.pallas_call(
         functools.partial(kernel, dims),
-        out_shape=[jax.ShapeDtypeStruct(slowness.shape, F32)] * 2,
+        out_shape=[pltpu.VMEM(slowness.shape, F32)] * 2,
         in_specs=[in_hbm] * 7,
-        out_specs=[in_hbm] * 2,
+        out_specs=[anywhere] * 2,
         scratch_shapes=scratch,
         compiler_params=pltpu.CompilerParams(
             collective_id=0, has_side_effects=True, vmem_limit_bytes=VMEM_BYTES
@@ -633,10 +634,10 @@
     return pl.pallas_call(
         publish,
         out_shape=[jax.ShapeDtypeStruct(slowness.shape, F32)] * 2,
-        in_specs=[in_hbm] * 2,
+        in_specs=[anywhere] * 2,
         out_specs=[in_hbm] * 2,
         scratch_shapes=[dma((2,))],
-        compiler_params=pltpu.CompilerParams(vmem_limit_bytes=VMEM_BYTES),
+        compiler_params=pltpu.CompilerParams(vmem_limit_bytes=1024 * 1024),
     )(image, grad)
 
 

time: 29.4 us -> 24.9 us (0.85)
  Pallas kernels: 28.4 us -> 23.8 us
    pallas_call x1, Pallas kernels: 5.09 us -> 0.67 us  [per_device(): pl.pallas_call(publish, out_shape=[jax.ShapeDtypeStruct(slowness.shape, F...]
where the time goes in v4:
time: 24.9 us; the launch traced here: 24.5 us
  Pallas kernels  23.8 us (96%)
  between operations  0.64 us (3%)
    pallas_call x1, Pallas kernels, per_device(): pl.pallas_call(functools.partial(kernel, dims), out_shape=[pltpu.VMEM(slo...  23.2 us
    pallas_call x1, Pallas kernels, per_device(): pl.pallas_call(publish, out_shape=[jax.ShapeDtypeStruct(slowness.shape, F...  0.67 us

profile of v4, /device:TPU:8, one launch (start us, length us, event | category | flops | bytes accessed | tf_op | source)
XLA Modules:
  0.0 24.5 jit_solution(13139001295886269669)
XLA Ops:
  0.6 23.2 %shard_map.86 = (f32[1,8,2048]{2,1,0:T(8,128)S(1)}, f32[1,8,2048]{2,1,0:T(8,128)S(1)}) custom-call(s32[2]{0:T(128)} %freq_hbm.1, bf16[2,2,8,2048]{3,2,1,0:T(8,128)(2,1)} %src_ref.1, bf16[2,2,8,2048]{3,2,1,0:T(8,128)(2,1)} %rcv_ref.1, f32[1,8,2048]{2,1,0:T(8,128)} %slow_ref.1, f32[1,8,2048]{2,1,0:T(8,128)} %coef_ref.1, s32[1,8,2048]{2,1,0:T(8,128)} %mask_ref.1, ...), custom_call_target="tpu_custom_call" | custom-call | tf_op jit(solution)/shard_map/pallas_call | solution.py:624
  23.8 0.7 %shard_map.87 = (f32[1,8,2048]{2,1,0:T(8,128)}, f32[1,8,2048]{2,1,0:T(8,128)}) custom-call(f32[1,8,2048]{2,1,0:T(8,128)S(1)} %get-tuple-element.4.image_in, f32[1,8,2048]{2,1,0:T(8,128)S(1)} %get-tuple-element.5.grad_in), custom_call_target="tpu_custom_call" | custom-call | tf_op jit(solution)/shard_map/pallas_call | solution.py:634

commit v5 on v4

--- a/solution.py
+++ b/solution.py
@@ -43,16 +43,20 @@
     return sin_out, cos_out
 
 
-def stencil(cur, prev, nxt):
-    row = lax.broadcasted_iota(jnp.int32, cur.shape, 0)
-    total = WEIGHTS[HALO] * (prev + nxt) - 2.0 * sum(WEIGHTS) * cur
-    for k in range(1, HALO):
-        inside = row >= k
-        near = jnp.where(inside, WEIGHTS[k], WEIGHTS[HALO - k])
-        far = jnp.where(inside, WEIGHTS[HALO - k], WEIGHTS[k])
-        mixed = near * cur + far * jnp.where(inside, prev, nxt)
-        total = total + pltpu.roll(mixed, HALO - k, 0)
-    return total
+def stencil_matrix(rows):
+    shape = (rows, 3 * rows)
+    out = lax.broadcasted_iota(jnp.int32, shape, 0)
+    source = lax.broadcasted_iota(jnp.int32, shape, 1)
+    tile = (source >= rows).astype(jnp.int32) + (source >= 2 * rows).astype(jnp.int32) - 1
+    source = source - (tile + 1) * rows
+    same = (out >> 3) == (source >> 3)
+    distance = jnp.abs(tile * HALO + (source & 7) - (out & 7))
+    weight = jnp.where(distance == 0, -2.0 * sum(WEIGHTS), 0.0)
+    for k in range(1, HALO + 1):
+        weight = jnp.where(distance == k, WEIGHTS[k], weight)
+    weight = jnp.where(same, weight, 0.0)
+    high = weight.astype(BF16)
+    return jnp.concatenate([high, (weight - high.astype(F32)).astype(BF16)], axis=0)
 
 
 def loop(count, body):
@@ -88,9 +92,9 @@
     state,
     adj,
     hbuf,
-    hlat,
     gbuf,
-    glat,
+    hmat,
+    gmat,
     qbuf,
     img,
     grad,
@@ -110,6 +114,7 @@
 ):
     D, LATS, L, layers, NF, C, nb, G, B, W = dims
     NFC = NF // C
+    R, RB = NFC * 32, NFC * 16
     me = lax.axis_index("depth")
     lat = lax.axis_index("lat")
     first = pl.multiple_of(me * W, B)
@@ -157,17 +162,20 @@
 
         @pl.when(jnp.logical_not(exists[way]))
         def _():
-            hlat[:, :, way] = jnp.zeros(hlat.shape[:2] + hlat.shape[3:], BF16)
-            glat[:, :, way] = jnp.zeros(glat.shape[:2] + glat.shape[3:], BF16)
+            for buf, rows in ((hbuf, R), (gbuf, RB)):
+                start = 0 if way == UP else 2 * rows
+                buf[:, :, start : start + rows, B : B + W] = jnp.zeros((L, C, rows, W), BF16)
 
     for way, start, slot in ((LEFT, 0, 0), (RIGHT, W + B, 1)):
 
         @pl.when(jnp.logical_not(exists[way]))
         def _():
-            hbuf[:, :, :, start : start + B] = jnp.zeros(hbuf.shape[:3] + (B,), BF16)
-            gbuf[:, :, :, start : start + B] = jnp.zeros(gbuf.shape[:3] + (B,), BF16)
+            for buf, rows in ((hbuf, R), (gbuf, RB)):
+                buf[:, :, rows : 2 * rows, start : start + B] = jnp.zeros((L, C, rows, B), BF16)
             band_edge[slot] = jnp.zeros((B, B), BF16)
 
+    hmat[...] = stencil_matrix(R)
+    gmat[...] = stencil_matrix(RB)
     for matrix in (band, band_t):
         for e in range(G):
             for r in range(G + 2):
@@ -226,13 +234,14 @@
             def _():
                 edge_copy(way).start()
 
-    def halo_copy(buf, lats, ssem, rsem, l, c, way):
+    def halo_copy(buf, rows, ssem, rsem, l, c, way):
+        own = pl.ds(rows, rows)
         if way in (UP, DOWN):
-            src = buf.at[l, c, :, pl.ds(B, W)]
-            dst = lats.at[l, c, opposite[way]]
+            src = buf.at[l, c, own, pl.ds(B, W)]
+            dst = buf.at[l, c, pl.ds(2 * rows if way == UP else 0, rows), pl.ds(B, W)]
         else:
-            src = buf.at[l, c, :, pl.ds(B if way == LEFT else W, B)]
-            dst = buf.at[l, c, :, pl.ds(W + B if way == LEFT else 0, B)]
+            src = buf.at[l, c, own, pl.ds(B if way == LEFT else W, B)]
+            dst = buf.at[l, c, own, pl.ds(W + B if way == LEFT else 0, B)]
         return pltpu.make_async_remote_copy(
             src_ref=src,
             dst_ref=dst,
@@ -256,8 +265,8 @@
             def _():
                 halo_copy(*args, l, c, opposite[way]).wait_recv()
 
-    forward = (hbuf, hlat, fsend, frecv)
-    backward = (gbuf, glat, bsend, brecv)
+    forward = (hbuf, R, fsend, frecv)
+    backward = (gbuf, RB, bsend, brecv)
 
     CW = min(W, 512)
     pieces = [slice(x, x + CW) for x in range(0, W, CW)]
@@ -280,7 +289,7 @@
         phase_im = re * sine + im * cosine
         phased[l, f, s, 0, :, cols] = phase_re
         phased[l, f, s, 1, :, cols] = phase_im
-        rows = pl.ds(pl.multiple_of((fi * 2 + s) * 16, 16), 16)
+        rows = pl.ds(pl.multiple_of(R + (fi * 2 + s) * 16, 16), 16)
         inner = slice(cols.start + B, cols.stop + B)
         hbuf[l, c, rows, inner] = jnp.concatenate([phase_re, phase_im], axis=0).astype(BF16)
 
@@ -295,13 +304,11 @@
 
         loop(NFC, one)
 
-    R, RB = NFC * 32, NFC * 16
-
     def band_groups(buf, matrix, l, groups, rows):
         for p in groups:
             left = p * G * B
             qbuf[: C * rows, left : left + G * B] = jnp.dot(
-                buf[l, :, :, left : left + (G + 2) * B].reshape(C * rows, (G + 2) * B),
+                buf[l, :, rows : 2 * rows, left : left + (G + 2) * B].reshape(C * rows, (G + 2) * B),
                 matrix[p].reshape((G + 2) * B, G * B),
                 preferred_element_type=F32,
             )
@@ -315,18 +322,23 @@
             wait_halo(args, l, c, (LEFT, RIGHT))
         band_groups(args[0], matrix, l, outer_groups, rows)
 
-    def lateral(buf, lats, l, c, row, cols):
-        rows = pl.ds(pl.multiple_of(row, 16), 16)
-        cur = buf[l, c, rows, cols.start + B : cols.stop + B].astype(F32)
-        prev = lats[l, c, UP, rows, cols].astype(F32)
-        nxt = lats[l, c, DOWN, rows, cols].astype(F32)
-        product = qbuf[pl.ds(pl.multiple_of(c * buf.shape[2] + row, 16), 16), cols]
-        return [
-            product[h] + stencil(cur[h], prev[h], nxt[h]) for h in (slice(0, 8), slice(8, 16))
-        ]
+    def add_stencil(buf, matrix, l, c, rows):
+        own = slice(c * rows, (c + 1) * rows)
+        for cols in pieces:
+            both = jnp.dot(
+                matrix[...],
+                buf[l, c, :, cols.start + B : cols.stop + B],
+                preferred_element_type=F32,
+            )
+            qbuf[own, cols] += both[:rows] + both[rows:]
+
+    def lateral(rows, c, row, cols):
+        product = qbuf[pl.ds(pl.multiple_of(c * rows + row, 16), 16), cols]
+        return product[:8], product[8:]
 
     def forward_finish(l, c):
         wait_halo(forward, l, c, (UP, DOWN))
+        add_stencil(hbuf, hmat, l, c, R)
 
         def one(fi):
             f = c * NFC + fi
@@ -334,7 +346,7 @@
                 coefs = coef[l, :, cols]
                 new = []
                 for s in range(2):
-                    q_re, q_im = lateral(hbuf, hlat, l, c, (fi * 2 + s) * 16, cols)
+                    q_re, q_im = lateral(R, c, (fi * 2 + s) * 16, cols)
                     re = phased[l, f, s, 0, :, cols] - coefs * q_im
                     im = phased[l, f, s, 1, :, cols] + coefs * q_re
                     new.append((re, im))
@@ -400,7 +412,7 @@
                 value = value + mu[part]
             adj[f, part, :, cols] = value
             scaled.append(coefs * value)
-        rows = pl.ds(pl.multiple_of(fi * 16, 16), 16)
+        rows = pl.ds(pl.multiple_of(RB + fi * 16, 16), 16)
         gbuf[l, c, rows, cols.start + B : cols.stop + B] = jnp.concatenate(
             scaled, axis=0
         ).astype(BF16)
@@ -414,12 +426,13 @@
 
     def backward_finish(l, c):
         wait_halo(backward, l, c, (UP, DOWN))
+        add_stencil(gbuf, gmat, l, c, RB)
 
         def one(fi):
             f = c * NFC + fi
             omega = omega_of(f)
             for cols in pieces:
-                t_re, t_im = lateral(gbuf, glat, l, c, fi * 16, cols)
+                t_re, t_im = lateral(RB, c, fi * 16, cols)
                 back_re = adj[f, 0, :, cols] + t_im
                 back_im = adj[f, 1, :, cols] - t_re
                 term = omega * (
@@ -600,10 +613,10 @@
         pltpu.VMEM((L, NF, 2, 2) + tile, F32),
         pltpu.VMEM((L, NF, 2) + tile, F32),
         pltpu.VMEM((NF, 2) + tile, F32),
-        pltpu.VMEM((L, C, R, W + 2 * B), BF16),
-        pltpu.VMEM((L, C, 2, R, W), BF16),
-        pltpu.VMEM((L, C, RB, W + 2 * B), BF16),
-        pltpu.VMEM((L, C, 2, RB, W), BF16),
+        pltpu.VMEM((L, C, 3 * R, W + 2 * B), BF16),
+        pltpu.VMEM((L, C, 3 * RB, W + 2 * B), BF16),
+        pltpu.VMEM((2 * R, 3 * R), BF16),
+        pltpu.VMEM((2 * RB, 3 * RB), BF16),
         pltpu.VMEM((C * R, W), F32),
         pltpu.VMEM((L,) + tile, F32),
         pltpu.VMEM((L,) + tile, F32),

time: 24.9 us -> 24.6 us (0.988)
  no operation moved by 1% of the time
where the time goes in v5:
time: 24.6 us; the launch traced here: 24.4 us
  Pallas kernels  23.8 us (97%)
  between operations  0.64 us (3%)
    pallas_call x1, Pallas kernels, per_device(): pl.pallas_call(functools.partial(kernel, dims), out_shape=[pltpu.VMEM(slo...  23.1 us
    pallas_call x1, Pallas kernels, per_device(): pl.pallas_call(publish, out_shape=[jax.ShapeDtypeStruct(slowness.shape, F...  0.67 us

profile of v5, /device:TPU:8, one launch (start us, length us, event | category | flops | bytes accessed | tf_op | source)
XLA Modules:
  0.0 24.4 jit_solution(12763304600552106881)
XLA Ops:
  0.6 23.1 %shard_map.86 = (f32[1,8,2048]{2,1,0:T(8,128)S(1)}, f32[1,8,2048]{2,1,0:T(8,128)S(1)}) custom-call(s32[2]{0:T(128)} %freq_hbm.1, bf16[2,2,8,2048]{3,2,1,0:T(8,128)(2,1)} %src_ref.1, bf16[2,2,8,2048]{3,2,1,0:T(8,128)(2,1)} %rcv_ref.1, f32[1,8,2048]{2,1,0:T(8,128)} %slow_ref.1, f32[1,8,2048]{2,1,0:T(8,128)} %coef_ref.1, s32[1,8,2048]{2,1,0:T(8,128)} %mask_ref.1, ...), custom_call_target="tpu_custom_call" | custom-call | tf_op jit(solution)/shard_map/pallas_call | solution.py:637
  23.7 0.7 %shard_map.87 = (f32[1,8,2048]{2,1,0:T(8,128)}, f32[1,8,2048]{2,1,0:T(8,128)}) custom-call(f32[1,8,2048]{2,1,0:T(8,128)S(1)} %get-tuple-element.4.image_in, f32[1,8,2048]{2,1,0:T(8,128)S(1)} %get-tuple-element.5.grad_in), custom_call_target="tpu_custom_call" | custom-call | tf_op jit(solution)/shard_map/pallas_call | solution.py:647

commit v6 on v5

--- a/solution.py
+++ b/solution.py
@@ -108,6 +108,8 @@
     erecv,
     osend,
     orecv,
+    xsend,
+    xrecv,
     own_sem,
     loc_sem,
     band_sem,
@@ -119,10 +121,20 @@
     lat = lax.axis_index("lat")
     first = pl.multiple_of(me * W, B)
     mine = pl.ds(first, W)
-    exists = {UP: lat > 0, DOWN: lat < LATS - 1, LEFT: me > 0, RIGHT: me < D - 1}
+    snake = LATS == 16
+
+    def partner_of(place):
+        if not snake:
+            return place
+        return place + lax.rem(place // 4, 2) * (2 - 4 * lax.rem(place // 2, 2))
+
+    partner = partner_of(lat)
+    swapped = partner != lat
+    stays = jnp.logical_not(swapped)
+    exists = {UP: partner > 0, DOWN: partner < LATS - 1, LEFT: me > 0, RIGHT: me < D - 1}
     target = {
-        UP: {"lat": lat - 1},
-        DOWN: {"lat": lat + 1},
+        UP: {"lat": partner_of(jnp.maximum(partner - 1, 0))},
+        DOWN: {"lat": partner_of(jnp.minimum(partner + 1, LATS - 1))},
         LEFT: {"depth": me - 1},
         RIGHT: {"depth": me + 1},
     }
@@ -131,20 +143,30 @@
     MESH = pl.DeviceIdType.MESH
 
     own_levels = pl.ds(me * layers, layers)
-    local = [
-        pltpu.make_async_copy(slow_ref.at[:, :, mine], slow.at[own_levels], loc_sem.at[0]),
-        pltpu.make_async_copy(src_ref.at[:, :, :, mine], fields.at[0], loc_sem.at[1]),
-        pltpu.make_async_copy(rcv_ref.at[:, :, :, mine], fields.at[1], loc_sem.at[2]),
-        pltpu.make_async_copy(coef_ref.at[:, :, mine], coef.at[own_levels], loc_sem.at[3]),
-        pltpu.make_async_copy(mask_ref.at[:, :, mine], mask.at[own_levels], loc_sem.at[4]),
-        pltpu.make_async_copy(freq_hbm, freq_ref, loc_sem.at[5]),
-    ] + [
+    tables = ((slow_ref, slow), (coef_ref, coef), (mask_ref, mask))
+    sources = (src_ref, rcv_ref)
+    local_tables = [
+        pltpu.make_async_copy(ref.at[:, :, mine], held.at[own_levels], loc_sem.at[a])
+        for a, (ref, held) in enumerate(tables)
+    ]
+    local_fields = [
+        pltpu.make_async_copy(sources[a].at[:, :, :, mine], fields.at[a], loc_sem.at[3 + a])
+        for a in range(2)
+    ]
+    freq_copy = pltpu.make_async_copy(freq_hbm, freq_ref, loc_sem.at[5])
+    band_copies = [
         pltpu.make_async_copy(
             band_ref.at[:, e], band.at[:, e : e + 3, :, e * B : (e + 1) * B], band_sem.at[e]
         )
         for e in range(G)
     ]
-    for copy in local:
+
+    @pl.when(stays)
+    def _():
+        for copy in local_tables + local_fields:
+            copy.start()
+
+    for copy in [freq_copy] + band_copies:
         copy.start()
 
     barrier = pltpu.get_barrier_semaphore()
@@ -158,6 +180,17 @@
         pl.semaphore_signal(
             barrier, inc=1, device_id={"depth": lax.rem(me + s, D)}, device_id_type=MESH
         )
+
+    @pl.when(swapped)
+    def _():
+        for s in range(D):
+            pl.semaphore_signal(
+                barrier,
+                inc=1,
+                device_id={"depth": lax.rem(me + s, D), "lat": partner},
+                device_id_type=MESH,
+            )
+
     for way in (UP, DOWN):
 
         @pl.when(jnp.logical_not(exists[way]))
@@ -183,10 +216,12 @@
                     matrix[:, r, :, e * B : (e + 1) * B] = jnp.zeros((nb // G, B, B), BF16)
 
     pl.semaphore_wait(
-        barrier, (D - 1) + exists[UP].astype(jnp.int32) + exists[DOWN].astype(jnp.int32)
+        barrier,
+        (D - 1)
+        + exists[UP].astype(jnp.int32)
+        + exists[DOWN].astype(jnp.int32)
+        + D * swapped.astype(jnp.int32),
     )
-
-    tables = ((slow_ref, slow), (coef_ref, coef), (mask_ref, mask))
 
     def table_copy(a, s):
         peer = lax.rem(me + s, D)
@@ -195,7 +230,7 @@
             dst_ref=tables[a][1].at[own_levels],
             send_sem=rsend.at[a, s],
             recv_sem=rrecv.at[a, s],
-            device_id={"depth": peer},
+            device_id={"depth": peer, "lat": partner},
             device_id_type=MESH,
         )
 
@@ -206,7 +241,7 @@
             dst_ref=tables[a][1].at[pl.ds(source * layers, layers)],
             send_sem=rsend.at[a, s],
             recv_sem=rrecv.at[a, s],
-            device_id={"depth": source},
+            device_id={"depth": source, "lat": partner},
             device_id_type=MESH,
         ).wait_recv()
 
@@ -221,13 +256,57 @@
             device_id_type=MESH,
         )
 
-    for a in (0, 1):
+    def field_copy(a, c):
+        chunk = pl.ds(c * NFC, NFC)
+        return pltpu.make_async_remote_copy(
+            src_ref=sources[a].at[chunk, :, :, mine],
+            dst_ref=fields.at[a, chunk],
+            send_sem=xsend.at[a, c],
+            recv_sem=xrecv.at[a, c],
+            device_id={"lat": partner},
+            device_id_type=MESH,
+        )
+
+    def send_table(a):
         for s in range(1, D):
             table_copy(a, s).start()
+        if snake:
+
+            @pl.when(swapped)
+            def _():
+                table_copy(a, 0).start()
+
+    def send_fields(c):
+        if snake:
+
+            @pl.when(swapped)
+            def _():
+                for a in range(2):
+                    field_copy(a, c).start()
+
+    def wait_fields(c):
+        if snake:
+
+            @pl.when(swapped)
+            def _():
+                for a in range(2):
+                    field_copy(a, c).wait_recv()
+
+        if c == 0:
+
+            @pl.when(stays)
+            def _():
+                for copy in local_fields:
+                    copy.wait()
+
+    send_table(0)
+    send_fields(0)
+    send_table(1)
+    for c in range(1, C):
+        send_fields(c)
 
     def late_sends():
-        for s in range(1, D):
-            table_copy(2, s).start()
+        send_table(2)
         for way in (LEFT, RIGHT):
 
             @pl.when(exists[way])
@@ -388,16 +467,18 @@
             dst_ref=results[a][1].at[l % layers, :, mine],
             send_sem=osend.at[a, l],
             recv_sem=orecv.at[a, l % layers, lax.rem(owner - me + D, D)],
-            device_id={"depth": owner},
+            device_id={"depth": owner, "lat": partner},
             device_id_type=MESH,
         )
 
     def deliver(a, l):
-        @pl.when(me == l // layers)
+        keeps = jnp.logical_and(me == l // layers, stays)
+
+        @pl.when(keeps)
         def _():
             own_copy(a, l).start()
 
-        @pl.when(me != l // layers)
+        @pl.when(jnp.logical_not(keeps))
         def _():
             out_copy(a, l).start()
 
@@ -459,7 +540,13 @@
         if l % layers == 0:
             s = lax.rem(me - l // layers + D, D)
 
-            @pl.when(s != 0)
+            keeps = jnp.logical_and(s == 0, stays)
+
+            @pl.when(keeps)
+            def _():
+                local_tables[a].wait()
+
+            @pl.when(jnp.logical_not(keeps))
             def _():
                 table_wait(a, s)
 
@@ -473,26 +560,23 @@
             value.astype(F32).T.astype(BF16)
         )
 
-    for copy in local[6:]:
+    for copy in band_copies:
         copy.wait()
     for j in range(nb):
         for k in range(3):
             if 0 <= j + k - 1 < nb:
                 transpose(j, k)
-    local[0].wait()
-    local[5].wait()
+    freq_copy.wait()
     arrive(0, 0)
     angles(0)
-    local[1].wait()
-    local[2].wait()
     for c in range(C):
+        wait_fields(c)
         first_phase(c)
         send_halo(forward, 0, c)
     late_sends()
     for l in range(1, L):
         arrive(0, l)
         angles(l)
-    local[3].wait()
     arrive(1, 0)
     for l in range(L):
         if l > 0:
@@ -513,7 +597,6 @@
                 send_halo(forward, l + 1, c)
         if l + 1 < L:
             deliver(0, l)
-    local[4].wait()
     for l in range(L):
         arrive(2, l)
     for c in range(C):
@@ -540,6 +623,16 @@
     for s in range(1, D):
         for a in range(3):
             table_copy(a, s).wait_send()
+    if snake:
+
+        @pl.when(swapped)
+        def _():
+            for a in range(3):
+                table_copy(a, 0).wait_send()
+            for a in range(2):
+                for c in range(C):
+                    field_copy(a, c).wait_send()
+
     for way in (LEFT, RIGHT):
 
         @pl.when(exists[way])
@@ -549,26 +642,36 @@
     for a in range(2):
         for l in range(L):
 
-            @pl.when(me == l // layers)
+            keeps = jnp.logical_and(me == l // layers, stays)
+
+            @pl.when(keeps)
             def _():
                 own_copy(a, l).wait()
 
-            @pl.when(me != l // layers)
+            @pl.when(jnp.logical_not(keeps))
             def _():
                 out_copy(a, l).wait_send()
+
+        def result_wait(i, s):
+            source = lax.rem(me - s + D, D)
+            theirs = pl.ds(pl.multiple_of(source * W, B), W)
+            pltpu.make_async_remote_copy(
+                src_ref=results[a][0].at[i],
+                dst_ref=results[a][1].at[i, :, theirs],
+                send_sem=osend.at[a, i],
+                recv_sem=orecv.at[a, i, s],
+                device_id={"depth": source, "lat": partner},
+                device_id_type=MESH,
+            ).wait_recv()
 
         for i in range(layers):
             for s in range(1, D):
-                source = lax.rem(me - s + D, D)
-                theirs = pl.ds(pl.multiple_of(source * W, B), W)
-                pltpu.make_async_remote_copy(
-                    src_ref=results[a][0].at[i],
-                    dst_ref=results[a][1].at[i, :, theirs],
-                    send_sem=osend.at[a, i],
-                    recv_sem=orecv.at[a, i, s],
-                    device_id={"depth": source},
-                    device_id_type=MESH,
-                ).wait_recv()
+                result_wait(i, s)
+            if snake:
+
+                @pl.when(swapped)
+                def _():
+                    result_wait(i, 0)
 
 
 def publish(image_in, grad_in, image_out, grad_out, sems):
@@ -630,6 +733,8 @@
         dma((2,)),
         dma((2, L)),
         dma((2, layers, D)),
+        dma((2, C)),
+        dma((2, C)),
         dma((2, layers)),
         dma((6,)),
         dma((G,)),

time: 24.6 us -> 28.6 us (1.16)
  Pallas kernels: 23.8 us -> 27.7 us
    pallas_call x1, Pallas kernels: 23.1 us -> 27 us  [per_device(): pl.pallas_call(functools.partial(kernel, dims), out_shape=[pltpu.VMEM(slo...]
where the time goes in v6:
time: 28.6 us; the launch traced here: 28.3 us
  Pallas kernels  27.7 us (97%)
  between operations  0.64 us (2%)
    pallas_call x1, Pallas kernels, per_device(): pl.pallas_call(functools.partial(kernel, dims), out_shape=[pltpu.VMEM(slo...  27 us
    pallas_call x1, Pallas kernels, per_device(): pl.pallas_call(publish, out_shape=[jax.ShapeDtypeStruct(slowness.shape, F...  0.67 us

profile of v6, /device:TPU:8, one launch (start us, length us, event | category | flops | bytes accessed | tf_op | source)
XLA Modules:
  0.0 28.3 jit_solution(9844361410384540828)
XLA Ops:
  0.6 27.0 %shard_map.86 = (f32[1,8,2048]{2,1,0:T(8,128)S(1)}, f32[1,8,2048]{2,1,0:T(8,128)S(1)}) custom-call(s32[2]{0:T(128)} %freq_hbm.1, bf16[2,2,8,2048]{3,2,1,0:T(8,128)(2,1)} %src_ref.1, bf16[2,2,8,2048]{3,2,1,0:T(8,128)(2,1)} %rcv_ref.1, f32[1,8,2048]{2,1,0:T(8,128)} %slow_ref.1, f32[1,8,2048]{2,1,0:T(8,128)} %coef_ref.1, s32[1,8,2048]{2,1,0:T(8,128)} %mask_ref.1, ...), custom_call_target="tpu_custom_call" | custom-call | tf_op jit(solution)/shard_map/pallas_call | solution.py:742
  27.6 0.7 %shard_map.87 = (f32[1,8,2048]{2,1,0:T(8,128)}, f32[1,8,2048]{2,1,0:T(8,128)}) custom-call(f32[1,8,2048]{2,1,0:T(8,128)S(1)} %get-tuple-element.4.image_in, f32[1,8,2048]{2,1,0:T(8,128)S(1)} %get-tuple-element.5.grad_in), custom_call_target="tpu_custom_call" | custom-call | tf_op jit(solution)/shard_map/pallas_call | solution.py:752

commit v7 on v5

--- a/solution.py
+++ b/solution.py
@@ -174,14 +174,6 @@
                 buf[:, :, rows : 2 * rows, start : start + B] = jnp.zeros((L, C, rows, B), BF16)
             band_edge[slot] = jnp.zeros((B, B), BF16)
 
-    hmat[...] = stencil_matrix(R)
-    gmat[...] = stencil_matrix(RB)
-    for matrix in (band, band_t):
-        for e in range(G):
-            for r in range(G + 2):
-                if not e <= r < e + 3:
-                    matrix[:, r, :, e * B : (e + 1) * B] = jnp.zeros((nb // G, B, B), BF16)
-
     pl.semaphore_wait(
         barrier, (D - 1) + exists[UP].astype(jnp.int32) + exists[DOWN].astype(jnp.int32)
     )
@@ -473,12 +465,15 @@
             value.astype(F32).T.astype(BF16)
         )
 
-    for copy in local[6:]:
-        copy.wait()
-    for j in range(nb):
-        for k in range(3):
-            if 0 <= j + k - 1 < nb:
-                transpose(j, k)
+    hmat[...] = stencil_matrix(R)
+    gmat[...] = stencil_matrix(RB)
+    for matrix in (band, band_t):
+        for e in range(G):
+            for r in range(G + 2):
+                if not e <= r < e + 3:
+                    matrix[:, r, :, e * B : (e + 1) * B] = jnp.zeros((nb // G, B, B), BF16)
+    inside = [(j, k) for j in range(nb) for k in range(3) if 0 <= j + k - 1 < nb]
+    half = len(inside) // 2
     local[0].wait()
     local[5].wait()
     arrive(0, 0)
@@ -494,10 +489,15 @@
         angles(l)
     local[3].wait()
     arrive(1, 0)
+    for copy in local[6:]:
+        copy.wait()
     for l in range(L):
         if l > 0:
             arrive(1, l)
         band_products(forward, band, l, R)
+        if l == 0:
+            for j, k in inside[:half]:
+                transpose(j, k)
         if l == L - 1:
             for way in (LEFT, RIGHT):
 
@@ -505,6 +505,8 @@
                 def _():
                     edge_copy(opposite[way]).wait_recv()
 
+            for j, k in inside[half:]:
+                transpose(j, k)
             transpose(-1, 2)
             transpose(nb, 0)
         for c in range(C):

time: 24.6 us -> 24.6 us (level)
  no operation moved by 1% of the time
where the time goes in v7:
time: 24.6 us; the launch traced here: 24.4 us
  Pallas kernels  23.8 us (97%)
  between operations  0.64 us (3%)
    pallas_call x1, Pallas kernels, per_device(): pl.pallas_call(functools.partial(kernel, dims), out_shape=[pltpu.VMEM(slo...  23.1 us
    pallas_call x1, Pallas kernels, per_device(): pl.pallas_call(publish, out_shape=[jax.ShapeDtypeStruct(slowness.shape, F...  0.67 us

profile of v7, /device:TPU:8, one launch (start us, length us, event | category | flops | bytes accessed | tf_op | source)
XLA Modules:
  0.0 24.4 jit_solution(17137327055860872047)
XLA Ops:
  0.6 23.1 %shard_map.86 = (f32[1,8,2048]{2,1,0:T(8,128)S(1)}, f32[1,8,2048]{2,1,0:T(8,128)S(1)}) custom-call(s32[2]{0:T(128)} %freq_hbm.1, bf16[2,2,8,2048]{3,2,1,0:T(8,128)(2,1)} %src_ref.1, bf16[2,2,8,2048]{3,2,1,0:T(8,128)(2,1)} %rcv_ref.1, f32[1,8,2048]{2,1,0:T(8,128)} %slow_ref.1, f32[1,8,2048]{2,1,0:T(8,128)} %coef_ref.1, s32[1,8,2048]{2,1,0:T(8,128)} %mask_ref.1, ...), custom_call_target="tpu_custom_call" | custom-call | tf_op jit(solution)/shard_map/pallas_call | solution.py:639
  23.7 0.7 %shard_map.87 = (f32[1,8,2048]{2,1,0:T(8,128)}, f32[1,8,2048]{2,1,0:T(8,128)}) custom-call(f32[1,8,2048]{2,1,0:T(8,128)S(1)} %get-tuple-element.4.image_in, f32[1,8,2048]{2,1,0:T(8,128)S(1)} %get-tuple-element.5.grad_in), custom_call_target="tpu_custom_call" | custom-call | tf_op jit(solution)/shard_map/pallas_call | solution.py:649

commit v8 on v5

--- a/solution.py
+++ b/solution.py
@@ -590,7 +590,7 @@
     nb, _, B, _ = band.shape
     W = width // D
     assert height == HALO and W == nb * B
-    C = 2 if NF % 2 == 0 else 1
+    C = 1
     NFC = NF // C
     G = 2 if nb % 2 == 0 else 1
     dims = (D, LATS, L, layers, NF, C, nb, G, B, W)

time: 24.6 us -> 25.5 us (1.037)
  Pallas kernels: 23.8 us -> 24.7 us
    pallas_call x1, Pallas kernels: 23.1 us -> 24.1 us  [per_device(): pl.pallas_call(functools.partial(kernel, dims), out_shape=[pltpu.VMEM(slo...]
where the time goes in v8:
time: 25.5 us; the launch traced here: 25.4 us
  Pallas kernels  24.7 us (97%)
  between operations  0.64 us (3%)
    pallas_call x1, Pallas kernels, per_device(): pl.pallas_call(functools.partial(kernel, dims), out_shape=[pltpu.VMEM(slo...  24.1 us
    pallas_call x1, Pallas kernels, per_device(): pl.pallas_call(publish, out_shape=[jax.ShapeDtypeStruct(slowness.shape, F...  0.67 us

profile of v8, /device:TPU:8, one launch (start us, length us, event | category | flops | bytes accessed | tf_op | source)
XLA Modules:
  0.0 25.4 jit_solution(10018191206827647575)
XLA Ops:
  0.6 24.1 %shard_map.86 = (f32[1,8,2048]{2,1,0:T(8,128)S(1)}, f32[1,8,2048]{2,1,0:T(8,128)S(1)}) custom-call(s32[2]{0:T(128)} %freq_hbm.1, bf16[2,2,8,2048]{3,2,1,0:T(8,128)(2,1)} %src_ref.1, bf16[2,2,8,2048]{3,2,1,0:T(8,128)(2,1)} %rcv_ref.1, f32[1,8,2048]{2,1,0:T(8,128)} %slow_ref.1, f32[1,8,2048]{2,1,0:T(8,128)} %coef_ref.1, s32[1,8,2048]{2,1,0:T(8,128)} %mask_ref.1, ...), custom_call_target="tpu_custom_call" | custom-call | tf_op jit(solution)/shard_map/pallas_call | solution.py:637
  24.7 0.7 %shard_map.87 = (f32[1,8,2048]{2,1,0:T(8,128)}, f32[1,8,2048]{2,1,0:T(8,128)}) custom-call(f32[1,8,2048]{2,1,0:T(8,128)S(1)} %get-tuple-element.4.image_in, f32[1,8,2048]{2,1,0:T(8,128)S(1)} %get-tuple-element.5.grad_in), custom_call_target="tpu_custom_call" | custom-call | tf_op jit(solution)/shard_map/pallas_call | solution.py:647

commit v9 on v5

--- a/solution.py
+++ b/solution.py
@@ -127,7 +127,7 @@
         RIGHT: {"depth": me + 1},
     }
     opposite = {UP: DOWN, DOWN: UP, LEFT: RIGHT, RIGHT: LEFT}
-    DIRS = (LEFT, RIGHT, UP, DOWN)
+    DIRS = (UP, DOWN, LEFT, RIGHT)
     MESH = pl.DeviceIdType.MESH
 
     own_levels = pl.ds(me * layers, layers)
@@ -221,13 +221,13 @@
             device_id_type=MESH,
         )
 
-    for a in (0, 1):
-        for s in range(1, D):
-            table_copy(a, s).start()
+    for s in range(1, D):
+        table_copy(0, s).start()
 
     def late_sends():
-        for s in range(1, D):
-            table_copy(2, s).start()
+        for a in (1, 2):
+            for s in range(1, D):
+                table_copy(a, s).start()
         for way in (LEFT, RIGHT):
 
             @pl.when(exists[way])

time: 24.6 us -> 24.6 us (level)
  no operation moved by 1% of the time
where the time goes in v9:
time: 24.6 us; the launch traced here: 24.4 us
  Pallas kernels  23.7 us (96%)
  between operations  0.64 us (3%)
    pallas_call x1, Pallas kernels, per_device(): pl.pallas_call(functools.partial(kernel, dims), out_shape=[pltpu.VMEM(slo...  23 us
    pallas_call x1, Pallas kernels, per_device(): pl.pallas_call(publish, out_shape=[jax.ShapeDtypeStruct(slowness.shape, F...  0.67 us

profile of v9, /device:TPU:8, one launch (start us, length us, event | category | flops | bytes accessed | tf_op | source)
XLA Modules:
  0.0 24.4 jit_solution(16942848378293493012)
XLA Ops:
  0.6 23.0 %shard_map.86 = (f32[1,8,2048]{2,1,0:T(8,128)S(1)}, f32[1,8,2048]{2,1,0:T(8,128)S(1)}) custom-call(s32[2]{0:T(128)} %freq_hbm.1, bf16[2,2,8,2048]{3,2,1,0:T(8,128)(2,1)} %src_ref.1, bf16[2,2,8,2048]{3,2,1,0:T(8,128)(2,1)} %rcv_ref.1, f32[1,8,2048]{2,1,0:T(8,128)} %slow_ref.1, f32[1,8,2048]{2,1,0:T(8,128)} %coef_ref.1, s32[1,8,2048]{2,1,0:T(8,128)} %mask_ref.1, ...), custom_call_target="tpu_custom_call" | custom-call | tf_op jit(solution)/shard_map/pallas_call | solution.py:637
  23.7 0.7 %shard_map.87 = (f32[1,8,2048]{2,1,0:T(8,128)}, f32[1,8,2048]{2,1,0:T(8,128)}) custom-call(f32[1,8,2048]{2,1,0:T(8,128)S(1)} %get-tuple-element.4.image_in, f32[1,8,2048]{2,1,0:T(8,128)S(1)} %get-tuple-element.5.grad_in), custom_call_target="tpu_custom_call" | custom-call | tf_op jit(solution)/shard_map/pallas_call | solution.py:647
